TPU v7x, 256 devices: a whole 4x4x8 slice. The times are simulated.
256 devices in a mesh: blk: 64 (over x_hi, z, y), tp: 4 (over x_lo, core).
Axes of the slice: x: 4 (x_hi: 2, x_lo: 2; x = x_hi * 2 + x_lo), y: 4, z: 8, core: 2. Of those that a mesh axis runs over, the one named last changes fastest.
Arguments:
- context_query_rows: bfloat16 [65536, 4096], P('blk', 'tp'), may hold values from -96 to 96
- context_key_rows: bfloat16 [65536, 1024], P('blk', 'tp'), may hold values from -8 to 8
- context_value_rows: bfloat16 [65536, 1024], P('blk', 'tp'), may hold values from -6 to 6
- block_lengths: int32 [64], replicated, may hold values from 512 to 1024, as said below
- scored_query_rows: bfloat16 [512, 4096], P('blk', 'tp'), may hold values from -96 to 96
- scored_positions: int32 [512], P('blk'), may hold values from 1024 to 65535, as said below
- out_weight: bfloat16 [4096, 4096], P('tp', 'blk'), may hold values from -0.09375 to 0.09375
Outputs:
- context_out: bfloat16 [65536, 4096], P('blk', 'tp')
- scored_out: bfloat16 [512, 4096], P('tp', 'blk')
Inputs may be any that keep to these rules, and one draw needn't show every extreme that they name: `block_lengths`: each block has 512 to 1024 live tokens; at least one block is full. `scored_positions`: each position is a live token of a block other than block 0.
All inputs are finite; a program needn't handle non-finite values.
Results may differ from a plain program's by a relative error of at most 0.015.
Values may be sent and summed in bfloat16 or wider, within the bound.
A program may use at most 320 MiB of HBM per device.

v0:
```python
import math

import jax
import jax.numpy as jnp
from jax import lax
from jax.sharding import PartitionSpec as P

QUERY_HEADS = 32
KEY_VALUE_HEADS = 8
HEAD_SIZE = 128


BLOCKED_SCORE = -1e30


def broadcast(shard, axis, root):
    mine = lax.axis_index(axis) == root
    return lax.psum(jnp.where(mine, shard, jnp.zeros_like(shard)), axis)


def attend(query_matrix, gathered_keys, gathered_values, allowed_mask):
    score_scale = 1.0 / math.sqrt(HEAD_SIZE)
    scores = (
        jnp.einsum(
            "rkgd,skd->rkgs", query_matrix, gathered_keys, preferred_element_type=jnp.float32
        )
        * score_scale
    )
    allowed = allowed_mask[:, None, None, :]
    masked = jnp.where(allowed, scores, BLOCKED_SCORE)
    row_peak = jnp.max(masked, axis=-1)
    weights = jnp.where(allowed, jnp.exp(masked - row_peak[..., None]), 0.0)
    weight_sum = jnp.sum(weights, axis=-1)
    weighted = jnp.einsum(
        "rkgs,skd->rkgd",
        weights.astype(jnp.bfloat16),
        gathered_values,
        preferred_element_type=jnp.float32,
    )
    return (row_peak, weight_sum, weighted)


def scale_rows(weighted, factor):
    full_shape = weighted.shape
    return (weighted.reshape(factor.shape + (HEAD_SIZE,)) * factor[..., None]).reshape(full_shape)


def divide_rows(weighted, weight_sum):
    full_shape = weighted.shape
    return (weighted.reshape(weight_sum.shape + (HEAD_SIZE,)) / weight_sum[..., None]).reshape(
        full_shape
    )


def local(
    context_query_rows,
    context_key_rows,
    context_value_rows,
    block_lengths,
    scored_query_rows,
    scored_positions,
    out_weight,
):
    block_rows = context_key_rows.shape[0]
    kv_local = context_key_rows.shape[1] // HEAD_SIZE
    query_groups = QUERY_HEADS // KEY_VALUE_HEADS
    kv_width = kv_local * HEAD_SIZE
    head_count = kv_local * query_groups
    own_block = lax.axis_index("blk")
    own_len = block_lengths[own_block]
    first_len = block_lengths[0]
    stacked = jnp.concatenate([context_key_rows, context_value_rows], axis=1)
    anchor = broadcast(stacked, "blk", 0)
    gathered_keys = jnp.concatenate([anchor[:, :kv_width], context_key_rows], axis=0).reshape(
        2 * block_rows, kv_local, HEAD_SIZE
    )
    gathered_values = jnp.concatenate([anchor[:, kv_width:], context_value_rows], axis=0).reshape(
        2 * block_rows, kv_local, HEAD_SIZE
    )
    positions_local = jnp.arange(block_rows, dtype=jnp.int32)
    anchor_live = (positions_local < first_len) & (own_block > 0)
    own_live = positions_local < own_len
    row_step = min(512, block_rows)

    def context_rows(starting_row):
        query_matrix = lax.dynamic_slice_in_dim(
            context_query_rows, starting_row, row_step, 0
        ).reshape(row_step, kv_local, query_groups, HEAD_SIZE)
        row_index = starting_row + jnp.arange(row_step, dtype=jnp.int32)
        local_mask = (positions_local[None, :] <= row_index[:, None]) & own_live[None, :]
        allowed_mask = jnp.concatenate(
            [jnp.broadcast_to(anchor_live[None, :], (row_step, block_rows)), local_mask], axis=1
        )
        row_peak, weight_sum, weighted = attend(
            query_matrix, gathered_keys, gathered_values, allowed_mask
        )
        return (
            (weighted / weight_sum[..., None])
            .reshape(row_step, head_count * HEAD_SIZE)
            .astype(jnp.bfloat16)
        )

    block_starts = jnp.arange(block_rows // row_step, dtype=jnp.int32) * row_step
    context_out = lax.map(context_rows, block_starts).reshape(block_rows, head_count * HEAD_SIZE)
    gathered_q, gathered_positions = (
        lax.all_gather(scored_query_rows, "blk", axis=0, tiled=True),
        lax.all_gather(scored_positions, "blk", axis=0, tiled=True),
    )
    query_count = gathered_q.shape[0]
    query_step = min(512, query_count)
    own_keys = context_key_rows.reshape(block_rows, kv_local, HEAD_SIZE)
    own_values = context_value_rows.reshape(block_rows, kv_local, HEAD_SIZE)
    absolute = own_block * block_rows + positions_local

    def query_block_terms(starting_row):
        query_matrix = gathered_q.reshape(query_step, kv_local, query_groups, HEAD_SIZE)
        allowed_mask = (absolute[None, :] <= gathered_positions[:, None]) & own_live[None, :]
        row_peak, weight_sum, weighted = attend(query_matrix, own_keys, own_values, allowed_mask)
        return (
            row_peak.reshape(query_step, head_count),
            weight_sum.reshape(query_step, head_count),
            weighted.reshape(query_step, head_count * HEAD_SIZE),
        )

    query_starts = jnp.arange(query_count // query_step, dtype=jnp.int32) * query_step
    peaks, sums, numers = lax.map(query_block_terms, query_starts)
    peaks = peaks.reshape(query_count, head_count)
    sums = sums.reshape(query_count, head_count)
    numers = numers.reshape(query_count, head_count * HEAD_SIZE)
    best_peak = lax.pmax(peaks, "blk")
    factor = jnp.exp(peaks - best_peak)
    merged_numer, merged_sums = (
        lax.psum_scatter(scale_rows(numers, factor), "blk", scatter_dimension=0, tiled=True),
        lax.psum_scatter(sums * factor, "blk", scatter_dimension=0, tiled=True),
    )
    attended = divide_rows(merged_numer, merged_sums).astype(jnp.bfloat16)
    projected = jnp.dot(
        lax.all_gather(attended, "blk", axis=0, tiled=True),
        out_weight,
        preferred_element_type=jnp.float32,
    )
    scored_out = lax.psum_scatter(
        projected.astype(jnp.bfloat16), "tp", scatter_dimension=0, tiled=True
    )
    return (context_out, scored_out)


def solution(mesh):
    in_specs = (
        P("blk", "tp"),
        P("blk", "tp"),
        P("blk", "tp"),
        P(),
        P("blk", "tp"),
        P("blk"),
        P("tp", "blk"),
    )
    out_specs = (P("blk", "tp"), P("tp", "blk"))
    return jax.shard_map(local, mesh=mesh, in_specs=in_specs, out_specs=out_specs, check_vma=False)
```

profile of v0, /device:TPU:1, one launch (start us, length us, event | category | flops | bytes accessed | tf_op | source)
XLA Modules:
  0.0 1758.4 jit_solution(16429772201588034940)
XLA Ops:
  7.2 0.0 all-gather.3.cloned.1.call-start
  7.2 0.7 all-gather.3.cloned.1.call-update
  7.9 0.0 reduce-scatter.8.cloned.1.call-start
  8.0 1.2 reshape.121
  9.1 1.2 copy.29
  10.4 1.3 fusion.53
  12.4 0.9 dynamic-update-slice
  13.3 24.1 %all-reduce = s32[512]{0:T(512)S(1)} all-reduce(s32[512]{0:T(512)S(1)} %dynamic-update-slice), channel_id=1, replica_groups=mesh['blk'=64,'tp'=4] {'blk'}, use_global_device_ids=true, to_apply=%add | all-reduce | flops 512 | bytes 4096
  37.4 1.3 fusion.54
  38.7 0.6 iota_compare_fusion.3
  39.3 0.8 compare_and_fusion
  40.2 85.3 %all-gather.3.cloned.1.call-done = bf16[512,1024]{1,0:T(8,128)(2,1)} async-done(((bf16[8,1024]{1,0:T(8,128)(2,1)}), bf16[512,1024]{1,0:T(8,128)(2,1)}) %all-gather.3.cloned.1.call-update) | async-done | bytes 1048592 | tf_op jit(solution)/shard_map/all_gather | solution.py:106
  125.5 1.5 copy.35
  127.0 7.3 fusion.34
  134.3 7.9 fusion.35
  142.3 299.7 %pmax.7 = f32[512,8]{0,1:T(8,128)S(1)} all-reduce(f32[512,8]{0,1:T(8,128)S(1)} %reshape.124), channel_id=1, replica_groups=mesh['blk'=64,'tp'=4] {'blk'}, use_global_device_ids=true, to_apply=%region_6.7 | all-reduce | flops 4096 | bytes 32768 | tf_op jit(solution)/shard_map/pmax | solution.py:130
  442.0 8.1 fusion.37
  450.1 0.3 bitcast_multiply_fusion
  450.4 1.8 copy.51
  452.3 0.0 all-reduce.4.cloned.1.call-start
  452.3 0.2 copy.28
  452.5 1.2 maximum_select_fusion
  453.7 0.0 all-reduce.4.cloned.1.call-update
  453.8 0.0 all-gather.5.cloned.1.call-start
  454.5 300.2 %all-reduce.1 = f32[512,8]{0,1:T(8,128)S(1)} all-reduce(f32[512,8]{0,1:T(8,128)S(1)} %get-tuple-element.141), channel_id=3, replica_groups=mesh['blk'=64,'tp'=4] {'blk'}, use_global_device_ids=true, to_apply=%region_9.10.clone | all-reduce | flops 4096 | bytes 32768
  754.7 0.1 constant_dynamic-slice_fusion.1
  754.8 65.2 %reduce-scatter.8.cloned.1.call-done = f32[8,1024]{1,0:T(8,128)} async-done(((f32[512,1024]{1,0:T(8,128)}), f32[8,1024]{1,0:T(8,128)}) %reduce-scatter.8.cloned.1.call-update) | async-done | bytes 32784
  819.9 0.9 copy.52
  820.9 0.1 fusion.40
  821.0 0.7 copy.40
  821.7 0.0 all-gather.5.cloned.1.call-update
  821.7 0.2 reduce-scatter.10.cloned.1.call-start
  822.0 695.2 %all-reduce.4.cloned.1.call-done = bf16[1024,512]{0,1:T(8,128)(2,1)} async-done(((bf16[1024,512]{0,1:T(8,128)(2,1)}), bf16[1024,512]{0,1:T(8,128)(2,1)}) %all-reduce.4.cloned.1.call-update) | async-done | bytes 1048592 | tf_op jit(solution)/shard_map/psum | solution.py:18
  1517.1 1.3 fusion.52
  1518.4 1.2 pad_maximum_fusion
  1519.6 0.7 copy.33
  1520.2 151.9 %all-gather.5.cloned.1.call-done = bf16[512,1024]{1,0:T(8,128)(2,1)} async-done(((bf16[8,1024]{1,0:T(8,128)(2,1)}), bf16[512,1024]{1,0:T(8,128)(2,1)}) %all-gather.5.cloned.1.call-update) | async-done | bytes 1048592 | tf_op jit(solution)/shard_map/all_gather | solution.py:138
  1672.1 1.7 convolution_convert_fusion
  1673.8 0.8 copy.55
  1674.5 0.0 reduce-scatter.10.cloned.1.call-update
  1674.6 75.9 %while.3 = (s32[]{:T(128)}, bf16[2,512,1024]{2,1,0:T(8,128)(2,1)}, s32[2]{0:T(128)S(1)}, bf16[1024,1024]{1,0:T(8,128)(2,1)}, bf16[2048,2,128]{2,0,1:T(8,128)(2,1...) while((s32[]{:T(128)}, bf16[2,512,1024]{2,1,0:T(8,128)(2,1)}, ...), condition=%wide.region_4.5_spmd.clone, body=%wide.region_1.4_spmd.clone.sunk | while | flops 4348450304 | bytes 49328828 | solution.py:104
  1674.6 0.6 dynamic_slice.18
  1677.1 1.5 constant_dynamic-slice_fusion.3
  1678.6 0.5 copy.66
  1679.2 0.7 iota_add_fusion.3
  1679.8 1.2 iota_compare_fusion.5
  1681.1 0.4 fusion.73
  1681.5 0.6 pad_add_fusion.2
  1682.1 19.4 %fusion.74 = (f32[512,2,4]{0,2,1:T(4,128)S(1)}, bf16[512,2,4,2048]{3,0,2,1:T(8,128)(2,1)}) fusion(pred[512,2048]{1,0:T(8,128)(4,1)S(1)} %pad_add_fusion.2, bf16[512,2,4,128]{0,3,2,1:T(8,128)(2,1)S(1)} %bitcast.108, bf16[2048,2,128]{2,0,1:T(8,128)(2,1)S(1)} %get-tuple-element.252), kind=kOutput, calls=%fused_computation.59.clone.1 | convolution fusion | flops 2197817344 | bytes 19939328 | tf_op jit(solution)/shard_map/while/body/eval_jaxpr/sub | solution.py:32
  1701.5 9.4 fusion.75
  1710.9 0.5 copy.67
  1711.5 1.0 constant_dynamic-update-slice_fusion.2
  1712.5 0.6 dynamic_slice.18
  1715.0 1.5 constant_dynamic-slice_fusion.3
  1716.6 0.5 copy.66
  1717.1 0.7 iota_add_fusion.3
  1717.8 1.2 iota_compare_fusion.5
  1719.0 0.4 fusion.73
  1719.4 0.6 pad_add_fusion.2
  1720.0 19.4 %fusion.74 = (f32[512,2,4]{0,2,1:T(4,128)S(1)}, bf16[512,2,4,2048]{3,0,2,1:T(8,128)(2,1)}) fusion(pred[512,2048]{1,0:T(8,128)(4,1)S(1)} %pad_add_fusion.2, bf16[512,2,4,128]{0,3,2,1:T(8,128)(2,1)S(1)} %bitcast.108, bf16[2048,2,128]{2,0,1:T(8,128)(2,1)S(1)} %get-tuple-element.252), kind=kOutput, calls=%fused_computation.59.clone.1 | convolution fusion | flops 2197817344 | bytes 19939328 | tf_op jit(solution)/shard_map/while/body/eval_jaxpr/sub | solution.py:32
  1739.4 9.4 fusion.75
  1748.9 0.5 copy.67
  1749.4 1.0 constant_dynamic-update-slice_fusion.2
  1750.5 1.4 copy.56
  (15 shorter events, 0.1 us)
Async XLA Ops:
  7.2 1664.9 %copy-start = (bf16[1024,64]{0,1:T(8,128)(2,1)S(1)}, bf16[1024,64]{0,1:T(8,128)(2,1)}, u32[]{:S(2)}) copy-start(bf16[1024,64]{0,1:T(8,128)(2,1)} %param.15) | copy-start | bytes 393220
  7.2 118.3 %all-gather.3.cloned.1.call-start = ((), (), s32[]{:S(2)}) async-start(), calls=%async_computation.3 | async-start | bytes 1064960 | tf_op jit(solution)/shard_map/all_gather | solution.py:106
  7.9 812.0 %reduce-scatter.8.cloned.1.call-start = ((), (), s32[]{:S(2)}) async-start(), calls=%async_computation.5 | async-start | bytes 2129920
  442.0 10.4 copy-start.1
  452.3 1064.9 %all-reduce.4.cloned.1.call-start = ((), (), s32[]{:S(2)}) async-start(), calls=%async_computation.2 | async-start | bytes 2097152 | tf_op jit(solution)/shard_map/psum | solution.py:18
  453.8 1218.3 %all-gather.5.cloned.1.call-start = ((), (), s32[]{:S(2)}) async-start(), calls=%async_computation.4 | async-start | bytes 1064960 | tf_op jit(solution)/shard_map/all_gather | solution.py:138
  821.7 928.7 %reduce-scatter.10.cloned.1.call-start = ((), (), s32[]{:S(2)}) async-start(), calls=%async_computation.6 | async-start | bytes 163840
Sparse Core Ops, SparseCore 0:
  11.8 113.7 all-gather.2
  452.4 367.5 reduce-scatter.7
  822.7 694.3 all-reduce.3
  1521.3 150.7 all-gather.4
  1674.7 20.9 reduce-scatter.9
where the time goes:
time: 1760 us
  waiting for transfers between devices  998 us (57%)
  blocking collectives  624 us (35%)
  matrix products  74.7 us (4%)
  local copies, waits for them, and re-layouts  23.8 us (1%)
  other arithmetic  17.9 us (1%)
    psum x1, waiting for transfers between devices, broadcast(): return lax.psum(jnp.where(mine, shard, jnp.zeros_like(shard)), axis)  695 us
    unnamed x2, blocking collectives  324 us
    pmax x1, blocking collectives, local(): best_peak = lax.pmax(peaks, 'blk')  300 us
    all_gather x1, waiting for transfers between devices, local(): lax.all_gather(attended, 'blk', axis=0, tiled=True)  152 us
    all_gather x1, waiting for transfers between devices, local(): lax.all_gather(scored_query_rows, 'blk', axis=0, tiled=True)  85.3 us
    unnamed x7, waiting for transfers between devices  65.9 us
    sub x2, matrix products, attend(): weights = jnp.where(allowed, jnp.exp(masked - row_peak[..., None]), 0.0)  38.8 us
  transfers between devices with their start and end apart: 5, of which 4 were waited for; matrix products, arithmetic and copies ran while one was open for 5% of the time, Pallas kernels for 0%

commit v1 on v0

v1 whole, which is shorter than its diff:
```python
import functools
import math

import jax
import jax.numpy as jnp
from jax import lax
from jax.experimental import pallas as pl
from jax.experimental.pallas import tpu as pltpu
from jax.sharding import PartitionSpec as P

BT = 1024
HEAD = 128
TOK = 8
PIECE = 4 * TOK
LOG2_SCALE = math.log2(math.e) / math.sqrt(HEAD)
NEG = -1e30
CHUNK = 256
TILE = 256
ROWS = 4 * TILE
MESH = pl.DeviceIdType.MESH
F32 = jnp.float32
BF16 = jnp.bfloat16


def dot_t(a, b):
    return lax.dot_general(a, b, (((1,), (1,)), ((), ())), preferred_element_type=F32)


def expand_keys(keys, values, live_len, filler_ref, kx, vx):
    live = lax.broadcasted_iota(jnp.int32, (BT, HEAD), 0) < live_len
    for g in range(2):
        cols = slice(g * HEAD, (g + 1) * HEAD)
        scaled = jnp.where(live, keys[:, cols].astype(F32), filler_ref[0:16, cols].astype(F32)[0:1]) * LOG2_SCALE
        high = scaled.astype(BF16)
        kx[g, :, 0:HEAD] = high
        kx[g, :, HEAD : 2 * HEAD] = (scaled - high.astype(F32)).astype(BF16)
        vx[g, :, 0:HEAD] = jnp.where(live, values[:, cols].astype(F32), 0.0).astype(BF16)
        vx[g, :, HEAD : 2 * HEAD] = jnp.where(live, 1.0, 0.0).astype(BF16)


def fold_max(m, s):
    for j in range(0, s.shape[1], HEAD):
        m = jnp.maximum(m, s[:, j : j + HEAD])
    return m


def context_queries(q_ref, g, r0):
    parts = [
        q_ref[r0 : r0 + TILE, pl.ds(pl.multiple_of(g * 512 + h * HEAD, HEAD), HEAD)] for h in range(4)
    ]
    q = jnp.concatenate(parts, axis=0)
    return jnp.concatenate([q, q], axis=1)


class Sems:
    def __init__(self, send, recv):
        self.send, self.recv, self.used = send, recv, 0

    def take(self):
        i = self.used
        self.used += 1
        return i


def merge(lses):
    best = functools.reduce(jnp.maximum, lses)
    terms = [jnp.exp2(l - best) for l in lses]
    total = functools.reduce(jnp.add, terms)
    return [t / total for t in terms], best + jnp.log2(total)


def lane_weights(w, lane):
    return jnp.concatenate(
        [jnp.broadcast_to(w[:, lane + h : lane + h + 1], (TOK, HEAD)) for h in range(4)], axis=0
    )


def kernel(
    dims,
    lengths,
    positions,
    q_hbm,
    k_hbm,
    v_hbm,
    qs_ref,
    w_ref,
    ctx_hbm,
    out_ref,
    q_ref,
    k_ref,
    v_ref,
    out_buf,
    kx,
    vx,
    akx,
    avx,
    s_buf,
    own_acc,
    own_peak,
    qa,
    qb,
    pos,
    ak,
    av,
    o0,
    o1,
    st0,
    st1,
    r0y,
    t0y,
    r1x,
    t1x,
    o0x,
    l0x,
    r0x,
    t0x,
    o1y,
    l1y,
    r1y,
    t1y,
    oz,
    lz,
    rz,
    tz,
    aa,
    ab,
    proj,
    rproj,
    send_sems,
    recv_sems,
    local_sems,
):
    NX, NZ, NY, NT = dims
    NB = NX * NZ * NY
    blk = lax.axis_index("blk")
    tp = lax.axis_index("tp")
    xh = blk // (NZ * NY)
    z = ((blk // NY) % NZ)
    y = ((blk) % NY)
    is_root = blk == 0
    other = NX - 1 - xh

    def at_x(v):
        return v * (NZ * NY) + z * NY + y

    def at_z(v):
        return xh * (NZ * NY) + v * NY + y

    def at_y(v):
        return xh * (NZ * NY) + z * NY + v

    zs = [((z + i) % NZ) for i in range(NZ)]
    ys = [((y + i) % NY) for i in range(NY)]
    zb = [((z + NZ - i) % NZ) for i in range(NZ)]
    yb = [((y + NY - i) % NY) for i in range(NY)]
    sems = Sems(send_sems, recv_sems)

    loads = [
        pltpu.make_async_copy(k_hbm, k_ref, local_sems.at[0]),
        pltpu.make_async_copy(v_hbm, v_ref, local_sems.at[1]),
        pltpu.make_async_copy(q_hbm, q_ref, local_sems.at[2]),
    ]
    for c in loads:
        c.start()

    barrier = pltpu.get_barrier_semaphore()

    def greet(device):
        pl.semaphore_signal(barrier, inc=1, device_id=device, device_id_type=MESH)

    for i in range(1, NZ):
        greet({"blk": at_z(zs[i])})
    for i in range(1, NY):
        greet({"blk": at_y(ys[i])})
    greet({"blk": at_x(other)})
    for i in range(1, NT):
        greet({"tp": ((tp + i) % NT)})

    @pl.when(jnp.logical_not(is_root))
    def _():
        greet({"blk": 0})

    near = NZ - 1 + NY - 1 + 1 + NT - 1

    def copy(src, dst, pair, device):
        return pltpu.make_async_remote_copy(
            src_ref=src, dst_ref=dst, send_sem=send_sems.at[pair], recv_sem=recv_sems.at[pair], device_id=device, device_id_type=MESH
        )

    sent = []

    def start(make):
        make().start()
        sent.append(make)

    class Gather:
        def __init__(self, a, b, extra=()):
            self.a, self.b = a, b
            self.first = tuple([a, b]) + tuple(extra)
            self.via_x = tuple([a]) + tuple(extra)
            self.p_z = [[sems.take() for _ in self.first] for _ in range(1, NZ)]
            self.p_ax = [sems.take() for _ in self.via_x]
            self.p_by = [sems.take() for _ in range(1, NY)]
            self.p_ay = [[sems.take() for _ in self.via_x] for _ in range(1, NY)]
            self.p_bx = sems.take()

        def start_z(self):
            for i in range(1, NZ):
                for ref, pair in zip(self.first, self.p_z[i - 1]):
                    start(lambda ref=ref, pair=pair, i=i: copy(ref.at[xh, z, y], ref.at[xh, z, y], pair, {"blk": at_z(zs[i])}))

        def wait_z(self):
            for i in range(1, NZ):
                for ref, pair in zip(self.first, self.p_z[i - 1]):
                    slot = ref.at[xh, zb[i], y]
                    copy(slot, slot, pair, {"blk": at_z(zs[i])}).wait_recv()

        def start_2(self):
            for ref, pair in zip(self.via_x, self.p_ax):
                start(lambda ref=ref, pair=pair: copy(ref.at[xh, :, y], ref.at[xh, :, y], pair, {"blk": at_x(other)}))
            for i in range(1, NY):
                start(lambda i=i: copy(self.b.at[xh, :, y], self.b.at[xh, :, y], self.p_by[i - 1], {"blk": at_y(ys[i])}))

        def wait_2(self):
            for ref, pair in zip(self.via_x, self.p_ax):
                slot = ref.at[other, :, y]
                copy(slot, slot, pair, {"blk": at_x(other)}).wait_recv()
            for i in range(1, NY):
                slot = self.b.at[xh, :, yb[i]]
                copy(slot, slot, self.p_by[i - 1], {"blk": at_y(ys[i])}).wait_recv()

        def start_3(self):
            for i in range(1, NY):
                for ref, pair in zip(self.via_x, self.p_ay[i - 1]):
                    start(lambda ref=ref, pair=pair, i=i: copy(ref.at[:, :, y], ref.at[:, :, y], pair, {"blk": at_y(ys[i])}))
            start(lambda: copy(self.b.at[xh], self.b.at[xh], self.p_bx, {"blk": at_x(other)}))

        def wait_3y(self, i):
            for ref, pair in zip(self.via_x, self.p_ay[i - 1]):
                slot = ref.at[:, :, yb[i]]
                copy(slot, slot, pair, {"blk": at_y(ys[i])}).wait_recv()

        def wait_3x(self):
            slot = self.b.at[other]
            copy(slot, slot, self.p_bx, {"blk": at_x(other)}).wait_recv()

    gather_q = Gather(qa, qb, (pos,))
    gather_kv = Gather(ak, av)
    gather_att = Gather(aa, ab)
    scatter = [sems.take() for _ in range(2)]
    p_y0 = [(sems.take(), sems.take()) for _ in range(1, NY)]
    p_x1 = [(sems.take(), sems.take())]
    p_x0 = [(sems.take(), sems.take())]
    p_y1 = [(sems.take(), sems.take()) for _ in range(1, NY)]
    p_z01 = [(sems.take(), sems.take()) for _ in range(1, NZ)]
    p_tp = [sems.take() for _ in range(1, NT)]

    q_piece = qs_ref[...].astype(F32)
    for g, ref in ((0, qa), (1, qb)):
        ref[xh, z, y] = jnp.concatenate(
            [q_piece[:, (g * 4 + h) * HEAD : (g * 4 + h + 1) * HEAD] for h in range(4)], axis=0
        ).astype(BF16)
    row = lax.broadcasted_iota(jnp.int32, (TOK, HEAD), 0)
    tile = jnp.zeros((TOK, HEAD), jnp.int32)
    for i in range(TOK):
        tile = jnp.where(row == i, positions[i], tile)
    pos[xh, z, y] = tile

    loads[0].wait()
    loads[1].wait()
    pl.semaphore_wait(barrier, near + jnp.where(is_root, NB - 1, 0))
    gather_q.start_z()

    share = BT // NB

    @pl.when(is_root)
    def _():
        ak[0, 0, 0] = k_ref[0:share, :]
        av[0, 0, 0] = v_ref[0:share, :]

        def hand(d, carry):
            rows = pl.ds(pl.multiple_of(d * share, share), share)
            dx, dz, dy = d // (NZ * NY), ((d // NY) % NZ), ((d) % NY)
            copy(k_ref.at[rows], ak.at[dx, dz, dy], scatter[0], {"blk": d}).start()
            copy(v_ref.at[rows], av.at[dx, dz, dy], scatter[1], {"blk": d}).start()
            return carry

        lax.fori_loop(1, NB, hand, 0)

    own_len = lengths[blk]
    anchor_len = jnp.where(is_root, 0, lengths[0])
    expand_keys(k_ref[...], v_ref[...], own_len, k_ref, kx, vx)
    loads[2].wait()

    def own_group(g, carry):
        prev = None
        for t in range(BT // TILE + 1):
            r0 = t * TILE
            here = t < BT // TILE
            if here:
                q = context_queries(q_ref, g, r0)
                m = jnp.full((ROWS, HEAD), NEG, F32)
            if prev is not None:
                acc = jnp.zeros((ROWS, 2 * HEAD), F32)
            for c in range(BT // CHUNK):
                cols = slice(c * CHUNK, (c + 1) * CHUNK)
                if here and c <= t:
                    s = dot_t(q, kx[g, cols, :])
                    if c == t:
                        i = lax.broadcasted_iota(jnp.int32, (4, TILE, CHUNK), 1).reshape(ROWS, CHUNK)
                        j = lax.broadcasted_iota(jnp.int32, (ROWS, CHUNK), 1)
                        s = jnp.where(j <= i, s, NEG)
                    s_buf[t % 2, :, cols] = s
                    m = fold_max(m, s)
                if prev is not None and c <= t - 1:
                    p = jnp.exp2(s_buf[(t - 1) % 2, :, cols] - prev).astype(BF16)
                    acc += jnp.dot(p, vx[g, cols, :], preferred_element_type=F32)
            if prev is not None:
                own_acc[g * 4 + t - 1] = acc
                own_peak[g * 4 + t - 1] = jnp.broadcast_to(prev, (ROWS, HEAD))
            if here:
                prev = jnp.max(m, axis=1, keepdims=True)

        @pl.when(g == 0)
        def _():
            gather_q.wait_z()
            gather_q.start_2()

        return carry

    lax.fori_loop(0, 2, own_group, 0)
    gather_q.wait_2()
    gather_q.start_3()

    @pl.when(jnp.logical_not(is_root))
    def _():
        copy(k_ref.at[0:share], ak.at[xh, z, y], scatter[0], {"blk": 0}).wait_recv()
        copy(v_ref.at[0:share], av.at[xh, z, y], scatter[1], {"blk": 0}).wait_recv()

    gather_kv.start_z()

    lane = lax.broadcasted_iota(jnp.int32, (TOK, HEAD), 1)
    dev0 = NX * NZ
    halves = NY // NX
    dev1 = NZ * NY // halves
    zpart = NZ // halves
    rows0 = dev0 * PIECE
    rows1 = dev1 * PIECE

    def scored_scores(q, limits, g, slot, count):
        rows = count * PIECE
        q = jnp.concatenate([q, q], axis=1)
        limits = jnp.concatenate([limits, limits], axis=2) - blk * BT
        m = jnp.full((rows, HEAD), NEG, F32)
        for c in range(BT // CHUNK):
            cols = slice(c * CHUNK, (c + 1) * CHUNK)
            s = dot_t(q, kx[g, cols, :]).reshape(count, 4, TOK, CHUNK)
            col = c * CHUNK + lax.broadcasted_iota(jnp.int32, (count, TOK, CHUNK), 2)
            ok = jnp.broadcast_to((col <= limits)[:, None], (count, 4, TOK, CHUNK))
            s = jnp.where(ok, s, NEG).reshape(rows, CHUNK)
            s_buf[slot, 0:rows, cols] = s
            m = fold_max(m, s)
        return jnp.max(m, axis=1, keepdims=True)

    def scored_values(peak, g, slot, count):
        rows = count * PIECE
        acc = jnp.zeros((rows, 2 * HEAD), F32)
        for c in range(BT // CHUNK):
            cols = slice(c * CHUNK, (c + 1) * CHUNK)
            p = jnp.exp2(s_buf[slot, 0:rows, cols] - peak).astype(BF16)
            acc += jnp.dot(p, vx[g, cols, :], preferred_element_type=F32)
        sums = acc[:, HEAD:]
        lse = (peak + jnp.log2(sums)).reshape(count, 4, TOK, HEAD)
        return (acc[:, :HEAD] / sums).astype(BF16), lse

    def stat_tile(lse, limits, devices, offsets):
        out = jnp.full((TOK, HEAD), NEG, F32)
        for d, offset in zip(devices, offsets):
            for h in range(4):
                out = jnp.where((lane == offset + h) & (limits[d] >= blk * BT), lse[d, h], out)
        return out

    for i in range(NY):
        yi = yb[i]
        xi = xh if i < halves else other
        z0 = (i % halves) * zpart
        if i > 0:
            gather_q.wait_3y(i)
        if i == halves:
            gather_q.wait_3x()
        q0 = qa[:, :, yi].reshape(rows0, HEAD)
        lim0 = pos[:, :, yi].reshape(dev0, TOK, HEAD)
        peak0 = scored_scores(q0, lim0, 0, 0, dev0)
        out0, lse0 = scored_values(peak0, 0, 0, dev0)
        o0[yi] = out0.reshape(NX, NZ, PIECE, HEAD)
        st0[yi] = stat_tile(
            lse0, lim0, range(dev0), [(d // NZ) * 64 + (d % NZ) * 8 for d in range(dev0)]
        )
        if i > 0:
            pairs = p_y0[NY - i - 1]
            start(lambda i=i, yi=yi, pair=pairs[0]: copy(o0.at[yi], r0y.at[NY - i - 1], pair, {"blk": at_y(yi)}))
            start(lambda i=i, yi=yi, pair=pairs[1]: copy(st0.at[yi], t0y.at[NY - i - 1], pair, {"blk": at_y(yi)}))
    for i in range(NY):
        xi = xh if i < halves else other
        z0 = (i % halves) * zpart
        q1 = qb[xi, z0 : z0 + zpart].reshape(rows1, HEAD)
        lim1 = pos[xi, z0 : z0 + zpart].reshape(dev1, TOK, HEAD)
        peak1 = scored_scores(q1, lim1, 1, 1, dev1)
        out1, lse1 = scored_values(peak1, 1, 1, dev1)
        o1[xi, z0 : z0 + zpart] = out1.reshape(zpart, NY, PIECE, HEAD)
        for yy in range(NY):
            devices = [zz * NY + yy for zz in range(zpart)]
            new = stat_tile(lse1, lim1, devices, [(z0 + zz) * 8 for zz in range(zpart)])
            if i % halves == 0:
                st1[xi, yy] = new
            else:
                st1[xi, yy] = jnp.maximum(st1[xi, yy], new)
    start(lambda: copy(o1.at[other], r1x, p_x1[0][0], {"blk": at_x(other)}))
    start(lambda: copy(st1.at[other], t1x, p_x1[0][1], {"blk": at_x(other)}))

    gather_kv.wait_z()
    gather_kv.start_2()

    def sums_1():
        for i in range(1, NY):
            copy(o0.at[y], r0y.at[i - 1], p_y0[i - 1][0], {"blk": at_y(ys[i])}).wait_recv()
            copy(st0.at[y], t0y.at[i - 1], p_y0[i - 1][1], {"blk": at_y(ys[i])}).wait_recv()
        ws, l0x[...] = merge([st0[y]] + [t0y[i] for i in range(NY - 1)])
        for a in range(NX):
            for b in range(NZ):
                at = a * 64 + b * 8
                total = o0[y, a, b].astype(F32) * lane_weights(ws[0], at)
                for i in range(NY - 1):
                    total += r0y[i, a, b].astype(F32) * lane_weights(ws[i + 1], at)
                o0x[a, b] = total.astype(BF16)
        start(lambda: copy(o0x.at[other], r0x, p_x0[0][0], {"blk": at_x(other)}))
        start(lambda: copy(l0x, t0x, p_x0[0][1], {"blk": at_x(other)}))
        copy(o1.at[xh], r1x, p_x1[0][0], {"blk": at_x(other)}).wait_recv()
        copy(st1.at[xh], t1x, p_x1[0][1], {"blk": at_x(other)}).wait_recv()
        for c in range(NY):
            ws, l1y[c] = merge([st1[xh, c], t1x[c]])
            for b in range(NZ):
                total = o1[xh, b, c].astype(F32) * lane_weights(ws[0], b * 8)
                total += r1x[b, c].astype(F32) * lane_weights(ws[1], b * 8)
                o1y[c, b] = total.astype(BF16)
        for i in range(1, NY):
            start(lambda i=i: copy(o1y.at[ys[i]], r1y.at[i - 1], p_y1[i - 1][0], {"blk": at_y(ys[i])}))
            start(lambda i=i: copy(l1y.at[ys[i]], t1y.at[i - 1], p_y1[i - 1][1], {"blk": at_y(ys[i])}))

    def sums_2():
        copy(o0x.at[xh], r0x, p_x0[0][0], {"blk": at_x(other)}).wait_recv()
        copy(l0x, t0x, p_x0[0][1], {"blk": at_x(other)}).wait_recv()

        def own_x(t):
            return jnp.where(xh == 0, t, pltpu.roll(t, 64, 1))

        ws, lse = merge([own_x(l0x[...]), own_x(t0x[...])])
        lz[0] = lse
        for b in range(NZ):
            total = o0x[xh, b].astype(F32) * lane_weights(ws[0], b * 8)
            total += r0x[b].astype(F32) * lane_weights(ws[1], b * 8)
            oz[b, 0] = total.astype(BF16)
        for i in range(1, NY):
            copy(o1y.at[y], r1y.at[i - 1], p_y1[i - 1][0], {"blk": at_y(ys[i])}).wait_recv()
            copy(l1y.at[y], t1y.at[i - 1], p_y1[i - 1][1], {"blk": at_y(ys[i])}).wait_recv()
        ws, lse = merge([l1y[y]] + [t1y[i] for i in range(NY - 1)])
        lz[1] = lse
        for b in range(NZ):
            total = o1y[y, b].astype(F32) * lane_weights(ws[0], b * 8)
            for i in range(NY - 1):
                total += r1y[i, b].astype(F32) * lane_weights(ws[i + 1], b * 8)
            oz[b, 1] = total.astype(BF16)
        for i in range(1, NZ):
            start(lambda i=i: copy(oz.at[zs[i]], rz.at[i - 1], p_z01[i - 1][0], {"blk": at_z(zs[i])}))
            start(lambda i=i: copy(lz, tz.at[i - 1], p_z01[i - 1][1], {"blk": at_z(zs[i])}))

    def sums_3():
        for i in range(1, NZ):
            copy(oz.at[z], rz.at[i - 1], p_z01[i - 1][0], {"blk": at_z(zs[i])}).wait_recv()
            copy(lz, tz.at[i - 1], p_z01[i - 1][1], {"blk": at_z(zs[i])}).wait_recv()
        for g, ref in ((0, aa), (1, ab)):
            ws, _ = merge([lz[g]] + [tz[i, g] for i in range(NZ - 1)])
            total = jnp.zeros((PIECE, HEAD), F32)
            for i in range(NZ):
                part = oz[z, g] if i == 0 else rz[i - 1, g]
                factor = jnp.concatenate(
                    [
                        jnp.broadcast_to(
                            jnp.sum(jnp.where(lane == z * 8 + h, ws[i], 0.0), axis=1, keepdims=True), (TOK, HEAD)
                        )
                        for h in range(4)
                    ],
                    axis=0,
                )
                total += part.astype(F32) * factor
            ref[xh, z, y] = total.astype(BF16)
        gather_att.start_z()

    gather_kv.wait_2()
    gather_kv.start_3()
    for i in range(1, NY):
        gather_kv.wait_3y(i)
    gather_kv.wait_3x()
    expand_keys(ak[...].reshape(BT, 2 * HEAD), av[...].reshape(BT, 2 * HEAD), anchor_len, k_ref, akx, avx)

    def anchor_group(g, carry):
        prev = None
        for t in range(BT // TILE + 1):
            r0 = t * TILE
            here = t < BT // TILE
            if here:
                q = context_queries(q_ref, g, r0)
                m = own_peak[g * 4 + t]
            if prev is not None:
                before = own_peak[g * 4 + t - 1]
                fade = jnp.exp2(before - prev)
                acc = own_acc[g * 4 + t - 1] * jnp.concatenate([fade, fade], axis=1)
            for c in range(BT // CHUNK):
                cols = slice(c * CHUNK, (c + 1) * CHUNK)
                if here:
                    s = dot_t(q, akx[g, cols, :])
                    s_buf[t % 2, :, cols] = s
                    m = fold_max(m, s)
                if prev is not None:
                    p = jnp.exp2(s_buf[(t - 1) % 2, :, cols] - prev).astype(BF16)
                    acc += jnp.dot(p, avx[g, cols, :], preferred_element_type=F32)
            if prev is not None:
                out = (acc[:, :HEAD] / acc[:, HEAD:]).astype(BF16)
                for h in range(4):
                    out_buf[g, (t - 1) * TILE : t * TILE, h * HEAD : (h + 1) * HEAD] = out[
                        h * TILE : (h + 1) * TILE
                    ]
            if here:
                prev = jnp.max(m, axis=1, keepdims=True)

        @pl.when(g == 0)
        def _():
            sums_1()

        return carry

    lax.fori_loop(0, 2, anchor_group, 0)
    stores = [
        pltpu.make_async_copy(out_buf.at[g], ctx_hbm.at[:, g * 512 : (g + 1) * 512], local_sems.at[3 + g])
        for g in range(2)
    ]
    for c in stores:
        c.start()
    sums_2()
    sums_3()
    gather_att.wait_z()
    gather_att.start_2()
    gather_att.wait_2()
    gather_att.start_3()
    for i in range(1, NY):
        gather_att.wait_3y(i)
    gather_att.wait_3x()

    total = jnp.zeros((NB, TOK, HEAD), F32)
    for g, ref in ((0, aa), (1, ab)):
        weights = jnp.concatenate(
            [w_ref[(g * 4 + h) * HEAD : (g * 4 + h + 1) * HEAD, :] for h in range(4)], axis=1
        )
        full = jnp.dot(ref[...].reshape(NB * PIECE, HEAD), weights, preferred_element_type=F32)
        full = full.reshape(NB, 4, TOK, 2 * HEAD)
        low = full[:, 0, :, :HEAD] + full[:, 2, :, HEAD:]
        high = full[:, 1, :, :HEAD] + full[:, 3, :, HEAD:]
        total += jnp.where(lax.broadcasted_iota(jnp.int32, (NB, TOK, HEAD), 2) < 64, low, high)
    total = total.reshape(NB * TOK, HEAD)
    total = total + pltpu.roll(total, 64, 1)
    per = NB * TOK // NT
    half = per // 2
    first = lax.broadcasted_iota(jnp.int32, (half, HEAD), 1) < 64
    for t in range(NT):
        proj[t] = jnp.where(first, total[t * per : t * per + half], total[t * per + half : (t + 1) * per]).astype(BF16)
    for i in range(1, NT):
        to = ((tp + i) % NT)
        start(lambda i=i, to=to: copy(proj.at[to], rproj.at[i - 1], p_tp[i - 1], {"tp": to}))
    result = proj[tp].astype(F32)
    for i in range(1, NT):
        copy(proj.at[tp], rproj.at[i - 1], p_tp[i - 1], {"tp": ((tp + i) % NT)}).wait_recv()
        result += rproj[i - 1].astype(F32)
    result = result.astype(BF16)
    out_ref[0:half, :] = result[:, 0:64]
    out_ref[half:per, :] = result[:, 64:128]

    for make in sent:
        make().wait_send()

    @pl.when(is_root)
    def _():
        def settle(d, carry):
            copy(k_ref.at[0:share], ak.at[0, 0, 0], scatter[0], {"blk": d}).wait_send()
            copy(v_ref.at[0:share], av.at[0, 0, 0], scatter[1], {"blk": d}).wait_send()
            return carry

        lax.fori_loop(1, NB, settle, 0)

    for c in stores:
        c.wait()


def solution(mesh, dims=(2, 8, 4, 4)):
    NX, NZ, NY, NT = dims
    NB = NX * NZ * NY
    vmem = pl.BlockSpec(memory_space=pltpu.VMEM)
    smem = pl.BlockSpec(memory_space=pltpu.SMEM)
    hbm = pl.BlockSpec(memory_space=pl.ANY)
    pieces = (NX, NZ, NY, PIECE, HEAD)
    anchor = (NX, NZ, NY, BT // NB, 2 * HEAD)
    per = NB * TOK // NT

    def local(q, k, v, lengths, q_scored, positions, weight):
        call = pl.pallas_call(
            functools.partial(kernel, dims),
            out_shape=(
                jax.ShapeDtypeStruct((BT, 1024), BF16),
                jax.ShapeDtypeStruct((per, 64), BF16),
            ),
            in_specs=[smem, smem, hbm, hbm, hbm, vmem, vmem],
            out_specs=(hbm, vmem),
            scratch_shapes=[
                pltpu.VMEM((BT, 1024), BF16),
                pltpu.VMEM((BT, 2 * HEAD), BF16),
                pltpu.VMEM((BT, 2 * HEAD), BF16),
                pltpu.VMEM((2, BT, 512), BF16),
                pltpu.VMEM((2, BT, 2 * HEAD), BF16),
                pltpu.VMEM((2, BT, 2 * HEAD), BF16),
                pltpu.VMEM((2, BT, 2 * HEAD), BF16),
                pltpu.VMEM((2, BT, 2 * HEAD), BF16),
                pltpu.VMEM((2, ROWS, BT), F32),
                pltpu.VMEM((8, ROWS, 2 * HEAD), F32),
                pltpu.VMEM((8, ROWS, HEAD), F32),
                pltpu.VMEM(pieces, BF16),
                pltpu.VMEM(pieces, BF16),
                pltpu.VMEM((NX, NZ, NY, TOK, HEAD), jnp.int32),
                pltpu.VMEM(anchor, BF16),
                pltpu.VMEM(anchor, BF16),
                pltpu.VMEM((NY, NX, NZ, PIECE, HEAD), BF16),
                pltpu.VMEM((NX, NZ, NY, PIECE, HEAD), BF16),
                pltpu.VMEM((NY, TOK, HEAD), F32),
                pltpu.VMEM((NX, NY, TOK, HEAD), F32),
                pltpu.VMEM((NY - 1, NX, NZ, PIECE, HEAD), BF16),
                pltpu.VMEM((NY - 1, TOK, HEAD), F32),
                pltpu.VMEM((NZ, NY, PIECE, HEAD), BF16),
                pltpu.VMEM((NY, TOK, HEAD), F32),
                pltpu.VMEM((NX, NZ, PIECE, HEAD), BF16),
                pltpu.VMEM((TOK, HEAD), F32),
                pltpu.VMEM((NZ, PIECE, HEAD), BF16),
                pltpu.VMEM((TOK, HEAD), F32),
                pltpu.VMEM((NY, NZ, PIECE, HEAD), BF16),
                pltpu.VMEM((NY, TOK, HEAD), F32),
                pltpu.VMEM((NY - 1, NZ, PIECE, HEAD), BF16),
                pltpu.VMEM((NY - 1, TOK, HEAD), F32),
                pltpu.VMEM((NZ, 2, PIECE, HEAD), BF16),
                pltpu.VMEM((2, TOK, HEAD), F32),
                pltpu.VMEM((NZ - 1, 2, PIECE, HEAD), BF16),
                pltpu.VMEM((NZ - 1, 2, TOK, HEAD), F32),
                pltpu.VMEM(pieces, BF16),
                pltpu.VMEM(pieces, BF16),
                pltpu.VMEM((NT, per // 2, HEAD), BF16),
                pltpu.VMEM((NT - 1, per // 2, HEAD), BF16),
                pltpu.SemaphoreType.DMA((160,)),
                pltpu.SemaphoreType.DMA((160,)),
                pltpu.SemaphoreType.DMA((5,)),
            ],
            compiler_params=pltpu.CompilerParams(
                collective_id=0, has_side_effects=True, vmem_limit_bytes=60 * 2**20
            ),
            name="star_attention",
        )
        return call(lengths, positions, q, k, v, q_scored, weight)

    in_specs = (P("blk", "tp"), P("blk", "tp"), P("blk", "tp"), P(), P("blk", "tp"), P("blk"), P("tp", "blk"))
    out_specs = (P("blk", "tp"), P("tp", "blk"))
    return jax.shard_map(local, mesh=mesh, in_specs=in_specs, out_specs=out_specs, check_vma=False)
```

time: 1760 us -> 109 us (0.06)
  waiting for transfers between devices: 998 us -> 0 us
  blocking collectives: 624 us -> 0 us
  Pallas kernels: 0 us -> 102 us
  matrix products: 74.7 us -> 0 us
  other arithmetic: 17.9 us -> 0 us
    psum x1 -> x0, waiting for transfers between devices: 695 us -> none  [broadcast(): return lax.psum(jnp.where(mine, shard, jnp.zeros_like(shard)), axis)]
    unnamed x2 -> x0, blocking collectives: 324 us -> none
    pmax x1 -> x0, blocking collectives: 300 us -> none  [local(): best_peak = lax.pmax(peaks, 'blk')]
    all_gather x2 -> x0, waiting for transfers between devices: 237 us -> none  [the longest x1 152 us: local(): lax.all_gather(attended, 'blk', axis=0, tiled=True)]
    pallas_call x0 -> x1, Pallas kernels: none -> 102 us  [local(): return call(lengths, positions, q, k, v, q_scored, weight)]
    unnamed x7 -> x0, waiting for transfers between devices: 65.9 us -> none
    sub x2 -> x0, matrix products: 38.8 us -> none  [attend(): weights = jnp.where(allowed, jnp.exp(masked - row_peak[..., None]), 0.0)]
    dot_general x5 -> x0, matrix products: 36 us -> none  [the longest x3 27 us: attend(): jnp.einsum('rkgs,skd->rkgd', weights.astype(jnp.bfloat16), gathered_value...]
  transfers between devices with their start and end apart: 5 -> 0, of which waited for: 4 -> 0; matrix products, arithmetic and copies ran while one was open for 5% -> 0% of each run, Pallas kernels for 0% -> 0%
where the time goes in v1:
time: 109 us
  Pallas kernels  102 us (94%)
  local copies, waits for them, and re-layouts  6.27 us (6%)
    pallas_call x1, Pallas kernels, local(): return call(lengths, positions, q, k, v, q_scored, weight)  102 us
    unnamed x2, local copies, waits for them, and re-layouts  4.82 us

profile of v1, /device:TPU:1, one launch (start us, length us, event | category | flops | bytes accessed | tf_op | source)
XLA Modules:
  0.0 108.7 jit_solution(10417040154855297883)
XLA Ops:
  0.6 1.7 %copy.9.w_ref = bf16[1024,64]{1,0:T(8,128)(2,1)} copy(bf16[1024,64]{0,1:T(8,128)(2,1)} %param.13) | data formatting | bytes 262144 | tf_op args[6]
  2.4 101.8 %star_attention.1 = (bf16[1024,1024]{1,0:T(8,128)(2,1)}, bf16[128,64]{1,0:T(8,128)(2,1)}) custom-call(s32[64]{0:T(128)} %lengths.1, s32[8]{0:T(128)} %positions.1, bf16[1024,1024]{1,0:T(8,128)(2,1)} %q_hbm.1, bf16[1024,256]{1,0:T(8,128)(2,1)} %k_hbm.1, bf16[1024,256]{1,0:T(8,128)(2,1)} %v_hbm.1, bf16[8,1024]{1,0:T(8,128)(2,1)} %qs_ref.1, ...), custom_call_target="tpu_custom_call" | custom-call | tf_op jit(solution)/shard_map/star_attention/pallas_call | solution.py:672
  104.1 1.4 %copy.10 = bf16[128,64]{0,1:T(8,128)(2,1)} copy(bf16[128,64]{1,0:T(8,128)(2,1)} %get-tuple-element.3) | data formatting | bytes 32768 | tf_op jit(solution)/shard_map/star_attention/pallas_call | solution.py:672
  105.6 3.1 %copy.12 = bf16[1024,1024]{1,0:T(8,128)(2,1)} copy(bf16[1024,1024]{1,0:T(8,128)(2,1)} %get-tuple-element.6) | data formatting | bytes 4194304

commit v2 on v1

--- a/solution.py
+++ b/solution.py
@@ -77,15 +77,18 @@
 
 def kernel(
     dims,
-    lengths,
-    positions,
+    lengths_hbm,
+    positions_hbm,
     q_hbm,
     k_hbm,
     v_hbm,
-    qs_ref,
-    w_ref,
+    qs_hbm,
+    w_hbm,
     ctx_hbm,
     out_ref,
+    lengths,
+    positions,
+    qs_ref,
     q_ref,
     k_ref,
     v_ref,
@@ -97,9 +100,11 @@
     s_buf,
     own_acc,
     own_peak,
+    qz,
     qa,
     qb,
     pos,
+    pos1,
     ak,
     av,
     o0,
@@ -122,10 +127,10 @@
     lz,
     rz,
     tz,
-    aa,
-    ab,
-    proj,
-    rproj,
+    att,
+    wt,
+    msg,
+    got,
     send_sems,
     recv_sems,
     local_sems,
@@ -134,10 +139,12 @@
     NB = NX * NZ * NY
     blk = lax.axis_index("blk")
     tp = lax.axis_index("tp")
-    xh = blk // (NZ * NY)
-    z = ((blk // NY) % NZ)
-    y = ((blk) % NY)
+    xh = lax.div(blk, NZ * NY)
+    z = lax.rem(lax.div(blk, NY), NZ)
+    y = lax.rem(blk, NY)
     is_root = blk == 0
+    HT = NT // NX
+    ZH = NZ // HT
     other = NX - 1 - xh
 
     def at_x(v):
@@ -149,38 +156,48 @@
     def at_y(v):
         return xh * (NZ * NY) + z * NY + v
 
-    zs = [((z + i) % NZ) for i in range(NZ)]
-    ys = [((y + i) % NY) for i in range(NY)]
-    zb = [((z + NZ - i) % NZ) for i in range(NZ)]
-    yb = [((y + NY - i) % NY) for i in range(NY)]
+    def at_xy(dx, dy):
+        return xs[dx] * (NZ * NY) + z * NY + ys[dy]
+
+    xs = [xh, NX - 1 - xh]
+    zs = [z] + [lax.rem(z + i, NZ) for i in range(1, NZ)]
+    ys = [y] + [lax.rem(y + i, NY) for i in range(1, NY)]
+    zb = [zs[(NZ - i) % NZ] for i in range(NZ)]
+    yb = [ys[(NY - i) % NY] for i in range(NY)]
     sems = Sems(send_sems, recv_sems)
 
+    barrier = pltpu.get_barrier_semaphore()
+
+    def greet(device):
+        pl.semaphore_signal(barrier, inc=1, device_id=device, device_id_type=MESH)
+
+    for i in range(1, NZ):
+        greet({"blk": at_z(zs[i])})
+    for dx in range(NX):
+        for dy in range(NY):
+            if dx or dy:
+                greet({"blk": at_xy(dx, dy)})
+    from_x = lax.div(tp, HT)
+    for dy in range(NY):
+        for dt in range(NT):
+            there = (from_x * (NZ * NY) + z * NY + ys[dy], lax.rem(tp + dt, NT))
+            if dy or dt:
+                greet(there)
+            else:
+                pl.when(from_x != xh)(functools.partial(greet, there))
+    near = NZ - 1 + NX * NY - 1 + NX * NY * HT - jnp.where(from_x == xh, 1, 0)
+
     loads = [
+        pltpu.make_async_copy(qs_hbm, qs_ref, local_sems.at[6]),
+        pltpu.make_async_copy(positions_hbm, positions, local_sems.at[7]),
         pltpu.make_async_copy(k_hbm, k_ref, local_sems.at[0]),
         pltpu.make_async_copy(v_hbm, v_ref, local_sems.at[1]),
         pltpu.make_async_copy(q_hbm, q_ref, local_sems.at[2]),
+        pltpu.make_async_copy(w_hbm, wt.at[xh, y], local_sems.at[5]),
     ]
+    loads.append(pltpu.make_async_copy(lengths_hbm, lengths, local_sems.at[8]))
     for c in loads:
         c.start()
-
-    barrier = pltpu.get_barrier_semaphore()
-
-    def greet(device):
-        pl.semaphore_signal(barrier, inc=1, device_id=device, device_id_type=MESH)
-
-    for i in range(1, NZ):
-        greet({"blk": at_z(zs[i])})
-    for i in range(1, NY):
-        greet({"blk": at_y(ys[i])})
-    greet({"blk": at_x(other)})
-    for i in range(1, NT):
-        greet({"tp": ((tp + i) % NT)})
-
-    @pl.when(jnp.logical_not(is_root))
-    def _():
-        greet({"blk": 0})
-
-    near = NZ - 1 + NY - 1 + 1 + NT - 1
 
     def copy(src, dst, pair, device):
         return pltpu.make_async_remote_copy(
@@ -193,71 +210,119 @@
         make().start()
         sent.append(make)
 
-    class Gather:
-        def __init__(self, a, b, extra=()):
-            self.a, self.b = a, b
-            self.first = tuple([a, b]) + tuple(extra)
-            self.via_x = tuple([a]) + tuple(extra)
-            self.p_z = [[sems.take() for _ in self.first] for _ in range(1, NZ)]
-            self.p_ax = [sems.take() for _ in self.via_x]
-            self.p_by = [sems.take() for _ in range(1, NY)]
-            self.p_ay = [[sems.take() for _ in self.via_x] for _ in range(1, NY)]
-            self.p_bx = sems.take()
+    class Queries:
+        def __init__(self):
+            self.p_z = [(sems.take(), sems.take()) for _ in range(1, NZ)]
+            self.p_ax = (sems.take(), sems.take())
+            self.p_bx = (sems.take(), sems.take())
+            self.p_ay = [(sems.take(), sems.take()) for _ in range(1, NY)]
+            self.p_by = [(sems.take(), sems.take()) for _ in range(1, NY)]
+
+        def refs(self, g, *at):
+            return (qa if g == 0 else qb).at[at], (pos if g == 0 else pos1).at[at]
+
+        def send(self, g, at, pairs, device):
+            for n in range(2):
+                start(lambda n=n: copy(self.refs(g, *at)[n], self.refs(g, *at)[n], pairs[n], device()))
+
+        def take(self, g, at, pairs):
+            for n in range(2):
+                ref = self.refs(g, *at)[n]
+                copy(ref, ref, pairs[n], {"blk": at_x(other)}).wait_recv()
 
         def start_z(self):
             for i in range(1, NZ):
-                for ref, pair in zip(self.first, self.p_z[i - 1]):
-                    start(lambda ref=ref, pair=pair, i=i: copy(ref.at[xh, z, y], ref.at[xh, z, y], pair, {"blk": at_z(zs[i])}))
+                start(lambda i=i: copy(qz.at[z], qz.at[z], self.p_z[i - 1][0], {"blk": at_z(zs[i])}))
+                start(
+                    lambda i=i: copy(
+                        pos.at[xh, z, y], pos.at[xh, z, y], self.p_z[i - 1][1], {"blk": at_z(zs[i])}
+                    )
+                )
 
         def wait_z(self):
             for i in range(1, NZ):
-                for ref, pair in zip(self.first, self.p_z[i - 1]):
-                    slot = ref.at[xh, zb[i], y]
-                    copy(slot, slot, pair, {"blk": at_z(zs[i])}).wait_recv()
+                slot = qz.at[zb[i]]
+                copy(slot, slot, self.p_z[i - 1][0], {"blk": at_z(zs[i])}).wait_recv()
+                slot = pos.at[xh, zb[i], y]
+                copy(slot, slot, self.p_z[i - 1][1], {"blk": at_z(zs[i])}).wait_recv()
+            qa[xh, :, y] = qz[:, 0]
+            qb[xh, :, y] = qz[:, 1]
+            pos1[xh, :, y] = pos[xh, :, y]
 
         def start_2(self):
-            for ref, pair in zip(self.via_x, self.p_ax):
-                start(lambda ref=ref, pair=pair: copy(ref.at[xh, :, y], ref.at[xh, :, y], pair, {"blk": at_x(other)}))
+            self.send(0, (xh, slice(None), y), self.p_ax, lambda: {"blk": at_x(other)})
             for i in range(1, NY):
-                start(lambda i=i: copy(self.b.at[xh, :, y], self.b.at[xh, :, y], self.p_by[i - 1], {"blk": at_y(ys[i])}))
+                self.send(1, (xh, slice(None), y), self.p_by[i - 1], lambda i=i: {"blk": at_y(ys[i])})
 
         def wait_2(self):
-            for ref, pair in zip(self.via_x, self.p_ax):
-                slot = ref.at[other, :, y]
-                copy(slot, slot, pair, {"blk": at_x(other)}).wait_recv()
+            self.take(0, (other, slice(None), y), self.p_ax)
             for i in range(1, NY):
-                slot = self.b.at[xh, :, yb[i]]
-                copy(slot, slot, self.p_by[i - 1], {"blk": at_y(ys[i])}).wait_recv()
+                self.take(1, (xh, slice(None), yb[i]), self.p_by[i - 1])
 
         def start_3(self):
             for i in range(1, NY):
-                for ref, pair in zip(self.via_x, self.p_ay[i - 1]):
-                    start(lambda ref=ref, pair=pair, i=i: copy(ref.at[:, :, y], ref.at[:, :, y], pair, {"blk": at_y(ys[i])}))
-            start(lambda: copy(self.b.at[xh], self.b.at[xh], self.p_bx, {"blk": at_x(other)}))
+                self.send(0, (slice(None), slice(None), y), self.p_ay[i - 1], lambda i=i: {"blk": at_y(ys[i])})
+            self.send(1, (xh,), self.p_bx, lambda: {"blk": at_x(other)})
 
         def wait_3y(self, i):
-            for ref, pair in zip(self.via_x, self.p_ay[i - 1]):
-                slot = ref.at[:, :, yb[i]]
-                copy(slot, slot, pair, {"blk": at_y(ys[i])}).wait_recv()
+            self.take(0, (slice(None), slice(None), yb[i]), self.p_ay[i - 1])
 
         def wait_3x(self):
-            slot = self.b.at[other]
-            copy(slot, slot, self.p_bx, {"blk": at_x(other)}).wait_recv()
-
-    gather_q = Gather(qa, qb, (pos,))
-    gather_kv = Gather(ak, av)
-    gather_att = Gather(aa, ab)
-    scatter = [sems.take() for _ in range(2)]
+            self.take(1, (other,), self.p_bx)
+
+    class Plane:
+        def __init__(self, a, b):
+            self.a, self.b = a, b
+            self.p_ax, self.p_bx = sems.take(), sems.take()
+            self.p_ay = [sems.take() for _ in range(1, NY)]
+            self.p_by = [sems.take() for _ in range(1, NY)]
+
+        def start_1(self):
+            start(lambda: copy(self.a(xh, y), self.a(xh, y), self.p_ax, {"blk": at_x(other)}))
+            for i in range(1, NY):
+                start(lambda i=i: copy(self.b(xh, y), self.b(xh, y), self.p_by[i - 1], {"blk": at_y(ys[i])}))
+
+        def wait_1(self):
+            copy(self.a(xh, y), self.a(other, y), self.p_ax, {"blk": at_x(other)}).wait_recv()
+            for i in range(1, NY):
+                copy(self.b(xh, y), self.b(xh, yb[i]), self.p_by[i - 1], {"blk": at_y(ys[i])}).wait_recv()
+
+        def start_2(self):
+            for i in range(1, NY):
+                start(
+                    lambda i=i: copy(self.a(slice(None), y), self.a(slice(None), y), self.p_ay[i - 1], {"blk": at_y(ys[i])})
+                )
+            start(lambda: copy(self.b(xh, slice(None)), self.b(xh, slice(None)), self.p_bx, {"blk": at_x(other)}))
+
+        def wait_2(self):
+            for i in range(1, NY):
+                copy(
+                    self.a(slice(None), y), self.a(slice(None), yb[i]), self.p_ay[i - 1], {"blk": at_y(ys[i])}
+                ).wait_recv()
+            copy(self.b(xh, slice(None)), self.b(other, slice(None)), self.p_bx, {"blk": at_x(other)}).wait_recv()
+
+    gather_q = Queries()
+    gather_kv = Plane(lambda a, b: ak.at[a, b], lambda a, b: av.at[a, b])
+    gather_w = Plane(lambda a, b: wt.at[a, b, :, 0:512], lambda a, b: wt.at[a, b, :, 512:1024])
+    p_plane = [[sems.take() for _ in range(NY)] for _ in range(NX)]
+    sems.used += 8
+    p_kv = (sems.take(), sems.take())
+    p_line = [(sems.take(), sems.take()) for _ in range(1, NZ)]
+    p_att = [sems.take() for _ in range(1, NZ)]
+    p_out = [sems.take() for _ in range(NX * NY * HT)]
+    p_from = sems.used
+    sems.used += NY * NT
     p_y0 = [(sems.take(), sems.take()) for _ in range(1, NY)]
-    p_x1 = [(sems.take(), sems.take())]
+    p_x1 = [sems.take() for _ in range(NY // NX + 1)]
     p_x0 = [(sems.take(), sems.take())]
     p_y1 = [(sems.take(), sems.take()) for _ in range(1, NY)]
     p_z01 = [(sems.take(), sems.take()) for _ in range(1, NZ)]
-    p_tp = [sems.take() for _ in range(1, NT)]
-
+
+    loads[0].wait()
+    loads[1].wait()
     q_piece = qs_ref[...].astype(F32)
-    for g, ref in ((0, qa), (1, qb)):
-        ref[xh, z, y] = jnp.concatenate(
+    for g in range(2):
+        qz[z, g] = jnp.concatenate(
             [q_piece[:, (g * 4 + h) * HEAD : (g * 4 + h + 1) * HEAD] for h in range(4)], axis=0
         ).astype(BF16)
     row = lax.broadcasted_iota(jnp.int32, (TOK, HEAD), 0)
@@ -266,31 +331,73 @@
         tile = jnp.where(row == i, positions[i], tile)
     pos[xh, z, y] = tile
 
-    loads[0].wait()
-    loads[1].wait()
-    pl.semaphore_wait(barrier, near + jnp.where(is_root, NB - 1, 0))
+    pl.semaphore_wait(barrier, near)
     gather_q.start_z()
-
-    share = BT // NB
+    loads[5].wait()
+    gather_w.start_1()
+    loads[2].wait()
+    loads[3].wait()
+
+    share = BT // (NX * NY)
+
+    def hand(dx, dy):
+        rows = pl.ds(pl.multiple_of((dx * NY + dy) * share, share), share)
+        device = {"blk": dx * (NZ * NY) + dy}
+        return [
+            pltpu.make_async_remote_copy(
+                src_ref=src.at[rows],
+                dst_ref=dst.at[dx, dy],
+                send_sem=send_sems.at[p_plane[dx][dy] + n * 8],
+                recv_sem=recv_sems.at[p_kv[n]],
+                device_id=device,
+                device_id_type=MESH,
+            )
+            for n, (src, dst) in enumerate(((k_ref, ak), (v_ref, av)))
+        ]
 
     @pl.when(is_root)
     def _():
-        ak[0, 0, 0] = k_ref[0:share, :]
-        av[0, 0, 0] = v_ref[0:share, :]
-
-        def hand(d, carry):
-            rows = pl.ds(pl.multiple_of(d * share, share), share)
-            dx, dz, dy = d // (NZ * NY), ((d // NY) % NZ), ((d) % NY)
-            copy(k_ref.at[rows], ak.at[dx, dz, dy], scatter[0], {"blk": d}).start()
-            copy(v_ref.at[rows], av.at[dx, dz, dy], scatter[1], {"blk": d}).start()
-            return carry
-
-        lax.fori_loop(1, NB, hand, 0)
-
+        ak[0, 0] = k_ref[0:share, :]
+        av[0, 0] = v_ref[0:share, :]
+        for dx in range(NX):
+            for dy in range(NY):
+                if dx or dy:
+                    for c in hand(dx, dy):
+                        c.start()
+
+    def line(i):
+        return [
+            pltpu.make_async_remote_copy(
+                src_ref=ref.at[xh, y],
+                dst_ref=ref.at[xh, y],
+                send_sem=send_sems.at[p_line[i - 1][n]],
+                recv_sem=recv_sems.at[p_kv[n]],
+                device_id={"blk": at_z(zs[i])},
+                device_id_type=MESH,
+            )
+            for n, ref in enumerate((ak, av))
+        ]
+
+    def arrived():
+        for c in line(1):
+            c.wait_recv()
+
+    def pass_on():
+        @pl.when((z == 0) & (blk > 0))
+        def _():
+            arrived()
+
+        @pl.when(z == 0)
+        def _():
+            for i in range(1, NZ):
+                for c in line(i):
+                    c.start()
+
+    loads[6].wait()
     own_len = lengths[blk]
     anchor_len = jnp.where(is_root, 0, lengths[0])
     expand_keys(k_ref[...], v_ref[...], own_len, k_ref, kx, vx)
-    loads[2].wait()
+    loads[4].wait()
 
     def own_group(g, carry):
         prev = None
@@ -320,24 +427,22 @@
                 own_peak[g * 4 + t - 1] = jnp.broadcast_to(prev, (ROWS, HEAD))
             if here:
                 prev = jnp.max(m, axis=1, keepdims=True)
-
-        @pl.when(g == 0)
-        def _():
-            gather_q.wait_z()
-            gather_q.start_2()
-
+            run_hooks(own_hooks, g, t)
         return carry
 
+    def second_step():
+        gather_q.wait_z()
+        gather_q.start_2()
+
+    def run_hooks(hooks, g, t):
+        for (at_g, at_t), hook in hooks.items():
+            if at_t == t:
+                pl.when(g == at_g)(hook)
+
+    own_hooks = {(0, 4): second_step, (1, 2): pass_on}
     lax.fori_loop(0, 2, own_group, 0)
     gather_q.wait_2()
     gather_q.start_3()
-
-    @pl.when(jnp.logical_not(is_root))
-    def _():
-        copy(k_ref.at[0:share], ak.at[xh, z, y], scatter[0], {"blk": 0}).wait_recv()
-        copy(v_ref.at[0:share], av.at[xh, z, y], scatter[1], {"blk": 0}).wait_recv()
-
-    gather_kv.start_z()
 
     lane = lax.broadcasted_iota(jnp.int32, (TOK, HEAD), 1)
     dev0 = NX * NZ
@@ -380,45 +485,50 @@
                 out = jnp.where((lane == offset + h) & (limits[d] >= blk * BT), lse[d, h], out)
         return out
 
-    for i in range(NY):
+    def scored_0(i):
         yi = yb[i]
+        lim0 = pos[:, :, yi].reshape(dev0, TOK, HEAD)
+        peak0 = scored_scores(qa[:, :, yi].reshape(rows0, HEAD), lim0, 0, 0, dev0)
+        out0, lse0 = scored_values(peak0, 0, 0, dev0)
+        o0[yi] = out0.reshape(NX, NZ, PIECE, HEAD)
+        st0[yi] = stat_tile(lse0, lim0, range(dev0), [(d // NZ) * 64 + (d % NZ) * 8 for d in range(dev0)])
+        if i > 0:
+            pairs = p_y0[NY - i - 1]
+            start(lambda pair=pairs[0]: copy(o0.at[yi], r0y.at[NY - i - 1], pair, {"blk": at_y(yi)}))
+            start(lambda pair=pairs[1]: copy(st0.at[yi], t0y.at[NY - i - 1], pair, {"blk": at_y(yi)}))
+
+    def scored_1(i):
         xi = xh if i < halves else other
         z0 = (i % halves) * zpart
-        if i > 0:
-            gather_q.wait_3y(i)
-        if i == halves:
-            gather_q.wait_3x()
-        q0 = qa[:, :, yi].reshape(rows0, HEAD)
-        lim0 = pos[:, :, yi].reshape(dev0, TOK, HEAD)
-        peak0 = scored_scores(q0, lim0, 0, 0, dev0)
-        out0, lse0 = scored_values(peak0, 0, 0, dev0)
-        o0[yi] = out0.reshape(NX, NZ, PIECE, HEAD)
-        st0[yi] = stat_tile(
-            lse0, lim0, range(dev0), [(d // NZ) * 64 + (d % NZ) * 8 for d in range(dev0)]
-        )
-        if i > 0:
-            pairs = p_y0[NY - i - 1]
-            start(lambda i=i, yi=yi, pair=pairs[0]: copy(o0.at[yi], r0y.at[NY - i - 1], pair, {"blk": at_y(yi)}))
-            start(lambda i=i, yi=yi, pair=pairs[1]: copy(st0.at[yi], t0y.at[NY - i - 1], pair, {"blk": at_y(yi)}))
-    for i in range(NY):
-        xi = xh if i < halves else other
-        z0 = (i % halves) * zpart
-        q1 = qb[xi, z0 : z0 + zpart].reshape(rows1, HEAD)
-        lim1 = pos[xi, z0 : z0 + zpart].reshape(dev1, TOK, HEAD)
-        peak1 = scored_scores(q1, lim1, 1, 1, dev1)
+        lim1 = pos1[xi, z0 : z0 + zpart].reshape(dev1, TOK, HEAD)
+        peak1 = scored_scores(qb[xi, z0 : z0 + zpart].reshape(rows1, HEAD), lim1, 1, 1, dev1)
         out1, lse1 = scored_values(peak1, 1, 1, dev1)
         o1[xi, z0 : z0 + zpart] = out1.reshape(zpart, NY, PIECE, HEAD)
         for yy in range(NY):
             devices = [zz * NY + yy for zz in range(zpart)]
             new = stat_tile(lse1, lim1, devices, [(z0 + zz) * 8 for zz in range(zpart)])
-            if i % halves == 0:
-                st1[xi, yy] = new
-            else:
-                st1[xi, yy] = jnp.maximum(st1[xi, yy], new)
-    start(lambda: copy(o1.at[other], r1x, p_x1[0][0], {"blk": at_x(other)}))
-    start(lambda: copy(st1.at[other], t1x, p_x1[0][1], {"blk": at_x(other)}))
-
-    gather_kv.wait_z()
+            st1[xi, yy] = new if i % halves == 0 else jnp.maximum(st1[xi, yy], new)
+
+    def send_1(n):
+        at = slice(n * zpart, (n + 1) * zpart)
+        start(lambda: copy(o1.at[other, at], r1x.at[at], p_x1[n], {"blk": at_x(other)}))
+
+    scored_0(0)
+    for i in range(halves):
+        scored_1(i)
+    order = [1, 3, 2] if NY == 4 else list(range(1, NY))
+    for n, i in enumerate(order):
+        gather_q.wait_3y(i)
+        scored_0(i)
+        if n == 0:
+            pl.when(z > 0)(arrived)
+            gather_kv.start_1()
+    gather_q.wait_3x()
+    for i in range(halves, NY):
+        scored_1(i)
+        send_1(i - halves)
+    start(lambda: copy(st1.at[other], t1x, p_x1[halves], {"blk": at_x(other)}))
+    gather_kv.wait_1()
     gather_kv.start_2()
 
     def sums_1():
@@ -435,8 +545,10 @@
                 o0x[a, b] = total.astype(BF16)
         start(lambda: copy(o0x.at[other], r0x, p_x0[0][0], {"blk": at_x(other)}))
         start(lambda: copy(l0x, t0x, p_x0[0][1], {"blk": at_x(other)}))
-        copy(o1.at[xh], r1x, p_x1[0][0], {"blk": at_x(other)}).wait_recv()
-        copy(st1.at[xh], t1x, p_x1[0][1], {"blk": at_x(other)}).wait_recv()
+        for n in range(halves):
+            at = slice(n * zpart, (n + 1) * zpart)
+            copy(o1.at[xh, at], r1x.at[at], p_x1[n], {"blk": at_x(other)}).wait_recv()
+        copy(st1.at[xh], t1x, p_x1[halves], {"blk": at_x(other)}).wait_recv()
         for c in range(NY):
             ws, l1y[c] = merge([st1[xh, c], t1x[c]])
             for b in range(NZ):
@@ -478,7 +590,7 @@
         for i in range(1, NZ):
             copy(oz.at[z], rz.at[i - 1], p_z01[i - 1][0], {"blk": at_z(zs[i])}).wait_recv()
             copy(lz, tz.at[i - 1], p_z01[i - 1][1], {"blk": at_z(zs[i])}).wait_recv()
-        for g, ref in ((0, aa), (1, ab)):
+        for g in range(2):
             ws, _ = merge([lz[g]] + [tz[i, g] for i in range(NZ - 1)])
             total = jnp.zeros((PIECE, HEAD), F32)
             for i in range(NZ):
@@ -493,15 +605,114 @@
                     axis=0,
                 )
                 total += part.astype(F32) * factor
-            ref[xh, z, y] = total.astype(BF16)
-        gather_att.start_z()
-
+            att[z, g] = total.astype(BF16)
+        for i in range(1, NZ):
+            start(lambda i=i: copy(att.at[z], att.at[z], p_att[i - 1], {"blk": at_z(zs[i])}))
+
+    def project():
+        for i in range(1, NZ):
+            copy(att.at[z], att.at[zb[i]], p_att[i - 1], {"blk": at_z(zs[i])}).wait_recv()
+        gather_w.wait_2()
+        rows = att[...].astype(F32)
+        rows = jnp.concatenate(
+            [rows[:, g, h * TOK : (h + 1) * TOK].reshape(NZ * TOK, HEAD) for g in range(2) for h in range(4)], axis=1
+        ).astype(BF16)
+        terms = dot_t(rows, wt[...].reshape(NX * NY * 64, 1024))
+        half = ZH * TOK // 2
+        first = lax.broadcasted_iota(jnp.int32, (half, HEAD), 1) < 64
+        for c in range(NX * NY):
+            for n in range(HT):
+                part = terms[n * 2 * half : (n + 1) * 2 * half, (c // 2) * HEAD : (c // 2 + 1) * HEAD]
+                top, low = part[0:half], part[half : 2 * half]
+                if c % 2 == 0:
+                    low = pltpu.roll(low, 64, 1)
+                else:
+                    top = pltpu.roll(top, 64, 1)
+                msg[c, n] = jnp.where(first, top, low).astype(BF16)
+        for n in range(HT):
+            to_t = xh * HT + n
+            for dx in range(NX):
+                for dy in range(NY):
+                    to_x, to_y = xs[dx], ys[dy]
+
+                    def send():
+                        return pltpu.make_async_remote_copy(
+                            src_ref=msg.at[to_x * NY + to_y, n],
+                            dst_ref=got.at[y, tp],
+                            send_sem=send_sems.at[p_out[(n * NX + dx) * NY + dy]],
+                            recv_sem=recv_sems.at[p_from + y * NT + tp],
+                            device_id=(to_x * (NZ * NY) + z * NY + to_y, to_t),
+                            device_id_type=MESH,
+                        )
+
+                    if dx or dy:
+                        send().start()
+                    else:
+                        pl.when(to_t != tp)(lambda: send().start())
+
+        @pl.when(from_x == xh)
+        def _():
+            got[y, tp] = msg[xh * NY + y, lax.rem(tp, HT)]
+
+    def finish():
+        for sy in range(NY):
+            for st in range(NT):
+
+                def await_one():
+                    pltpu.make_async_remote_copy(
+                        src_ref=msg.at[0, 0],
+                        dst_ref=got.at[sy, st],
+                        send_sem=send_sems.at[p_out[0]],
+                        recv_sem=recv_sems.at[p_from + sy * NT + st],
+                        device_id=(blk, tp),
+                        device_id_type=MESH,
+                    ).wait_recv()
+
+                pl.when((from_x != xh) | (sy != y) | (st != tp))(await_one)
+        sums = []
+        for sy in range(NY):
+            total = got[sy, 0].astype(F32)
+            for st in range(1, NT):
+                total += got[sy, st].astype(F32)
+            sums.append((total, pltpu.roll(total, 64, 1)))
+        blocks = []
+        for zz in range(ZH):
+            for sy in range(NY):
+                whole = sums[sy][zz // (ZH // 2)]
+                at = (zz % (ZH // 2)) * TOK
+                blocks.append(whole[at : at + TOK])
+        result = jnp.concatenate(blocks, axis=0).T
+        out_ref[...] = result[0:64].astype(BF16)
+        for n in range(HT):
+            for dx in range(NX):
+                for dy in range(NY):
+
+                    def settle():
+                        pltpu.make_async_remote_copy(
+                            src_ref=msg.at[0, n],
+                            dst_ref=got.at[y, tp],
+                            send_sem=send_sems.at[p_out[(n * NX + dx) * NY + dy]],
+                            recv_sem=recv_sems.at[p_from],
+                            device_id=(blk, tp),
+                            device_id_type=MESH,
+                        ).wait_send()
+
+                    if dx or dy:
+                        settle()
+                    else:
+                        pl.when(xh * HT + n != tp)(settle)
+
+    sums_1()
+    sums_2()
     gather_kv.wait_2()
-    gather_kv.start_3()
-    for i in range(1, NY):
-        gather_kv.wait_3y(i)
-    gather_kv.wait_3x()
+    gather_w.wait_1()
+    gather_w.start_2()
     expand_keys(ak[...].reshape(BT, 2 * HEAD), av[...].reshape(BT, 2 * HEAD), anchor_len, k_ref, akx, avx)
+    stores = [
+        pltpu.make_async_copy(out_buf.at[g], ctx_hbm.at[:, g * 512 : (g + 1) * 512], local_sems.at[3 + g])
+        for g in range(2)
+    ]
+    anchor_hooks = {(0, 2): sums_3, (1, 0): stores[0].start, (1, 2): project}
 
     def anchor_group(g, carry):
         prev = None
@@ -533,81 +744,40 @@
             if here:
                 prev = jnp.max(m, axis=1, keepdims=True)
 
-        @pl.when(g == 0)
-        def _():
-            sums_1()
-
+            run_hooks(anchor_hooks, g, t)
         return carry
 
     lax.fori_loop(0, 2, anchor_group, 0)
-    stores = [
-        pltpu.make_async_copy(out_buf.at[g], ctx_hbm.at[:, g * 512 : (g + 1) * 512], local_sems.at[3 + g])
-        for g in range(2)
-    ]
-    for c in stores:
-        c.start()
-    sums_2()
-    sums_3()
-    gather_att.wait_z()
-    gather_att.start_2()
-    gather_att.wait_2()
-    gather_att.start_3()
-    for i in range(1, NY):
-        gather_att.wait_3y(i)
-    gather_att.wait_3x()
-
-    total = jnp.zeros((NB, TOK, HEAD), F32)
-    for g, ref in ((0, aa), (1, ab)):
-        weights = jnp.concatenate(
-            [w_ref[(g * 4 + h) * HEAD : (g * 4 + h + 1) * HEAD, :] for h in range(4)], axis=1
-        )
-        full = jnp.dot(ref[...].reshape(NB * PIECE, HEAD), weights, preferred_element_type=F32)
-        full = full.reshape(NB, 4, TOK, 2 * HEAD)
-        low = full[:, 0, :, :HEAD] + full[:, 2, :, HEAD:]
-        high = full[:, 1, :, :HEAD] + full[:, 3, :, HEAD:]
-        total += jnp.where(lax.broadcasted_iota(jnp.int32, (NB, TOK, HEAD), 2) < 64, low, high)
-    total = total.reshape(NB * TOK, HEAD)
-    total = total + pltpu.roll(total, 64, 1)
-    per = NB * TOK // NT
-    half = per // 2
-    first = lax.broadcasted_iota(jnp.int32, (half, HEAD), 1) < 64
-    for t in range(NT):
-        proj[t] = jnp.where(first, total[t * per : t * per + half], total[t * per + half : (t + 1) * per]).astype(BF16)
-    for i in range(1, NT):
-        to = ((tp + i) % NT)
-        start(lambda i=i, to=to: copy(proj.at[to], rproj.at[i - 1], p_tp[i - 1], {"tp": to}))
-    result = proj[tp].astype(F32)
-    for i in range(1, NT):
-        copy(proj.at[tp], rproj.at[i - 1], p_tp[i - 1], {"tp": ((tp + i) % NT)}).wait_recv()
-        result += rproj[i - 1].astype(F32)
-    result = result.astype(BF16)
-    out_ref[0:half, :] = result[:, 0:64]
-    out_ref[half:per, :] = result[:, 64:128]
-
+    stores[1].start()
+    finish()
     for make in sent:
         make().wait_send()
 
     @pl.when(is_root)
     def _():
-        def settle(d, carry):
-            copy(k_ref.at[0:share], ak.at[0, 0, 0], scatter[0], {"blk": d}).wait_send()
-            copy(v_ref.at[0:share], av.at[0, 0, 0], scatter[1], {"blk": d}).wait_send()
-            return carry
-
-        lax.fori_loop(1, NB, settle, 0)
+        for dx in range(NX):
+            for dy in range(NY):
+                if dx or dy:
+                    for c in hand(dx, dy):
+                        c.wait_send()
+
+    @pl.when(z == 0)
+    def _():
+        for i in range(1, NZ):
+            for c in line(i):
+                c.wait_send()
 
     for c in stores:
         c.wait()
 
 
-def solution(mesh, dims=(2, 8, 4, 4)):
+def solution(mesh, dims=(2, 8, 4, 4), vlim=44):
     NX, NZ, NY, NT = dims
     NB = NX * NZ * NY
     vmem = pl.BlockSpec(memory_space=pltpu.VMEM)
-    smem = pl.BlockSpec(memory_space=pltpu.SMEM)
     hbm = pl.BlockSpec(memory_space=pl.ANY)
     pieces = (NX, NZ, NY, PIECE, HEAD)
-    anchor = (NX, NZ, NY, BT // NB, 2 * HEAD)
+    anchor = (NX, NY, BT // (NX * NY), 2 * HEAD)
     per = NB * TOK // NT
 
     def local(q, k, v, lengths, q_scored, positions, weight):
@@ -615,11 +785,14 @@
             functools.partial(kernel, dims),
             out_shape=(
                 jax.ShapeDtypeStruct((BT, 1024), BF16),
-                jax.ShapeDtypeStruct((per, 64), BF16),
+                jax.ShapeDtypeStruct((64, per), BF16),
             ),
-            in_specs=[smem, smem, hbm, hbm, hbm, vmem, vmem],
+            in_specs=[pl.BlockSpec(memory_space=pltpu.HBM)] * 7,
             out_specs=(hbm, vmem),
             scratch_shapes=[
+                pltpu.SMEM((NB,), jnp.int32),
+                pltpu.SMEM((TOK,), jnp.int32),
+                pltpu.VMEM((TOK, 1024), BF16),
                 pltpu.VMEM((BT, 1024), BF16),
                 pltpu.VMEM((BT, 2 * HEAD), BF16),
                 pltpu.VMEM((BT, 2 * HEAD), BF16),
@@ -631,8 +804,10 @@
                 pltpu.VMEM((2, ROWS, BT), F32),
                 pltpu.VMEM((8, ROWS, 2 * HEAD), F32),
                 pltpu.VMEM((8, ROWS, HEAD), F32),
+                pltpu.VMEM((NZ, 2, PIECE, HEAD), BF16),
                 pltpu.VMEM(pieces, BF16),
                 pltpu.VMEM(pieces, BF16),
+                pltpu.VMEM((NX, NZ, NY, TOK, HEAD), jnp.int32),
                 pltpu.VMEM((NX, NZ, NY, TOK, HEAD), jnp.int32),
                 pltpu.VMEM(anchor, BF16),
                 pltpu.VMEM(anchor, BF16),
@@ -656,20 +831,21 @@
                 pltpu.VMEM((2, TOK, HEAD), F32),
                 pltpu.VMEM((NZ - 1, 2, PIECE, HEAD), BF16),
                 pltpu.VMEM((NZ - 1, 2, TOK, HEAD), F32),
-                pltpu.VMEM(pieces, BF16),
-                pltpu.VMEM(pieces, BF16),
-                pltpu.VMEM((NT, per // 2, HEAD), BF16),
-                pltpu.VMEM((NT - 1, per // 2, HEAD), BF16),
-                pltpu.SemaphoreType.DMA((160,)),
-                pltpu.SemaphoreType.DMA((160,)),
-                pltpu.SemaphoreType.DMA((5,)),
+                pltpu.VMEM((NZ, 2, PIECE, HEAD), BF16),
+                pltpu.VMEM((NX, NY, 64, 1024), BF16),
+                pltpu.VMEM((NX * NY, NT // NX, NZ * NX // NT * TOK // 2, HEAD), BF16),
+                pltpu.VMEM((NY, NT, NZ * NX // NT * TOK // 2, HEAD), BF16),
+                pltpu.SemaphoreType.DMA((200,)),
+                pltpu.SemaphoreType.DMA((200,)),
+                pltpu.SemaphoreType.DMA((9,)),
             ],
             compiler_params=pltpu.CompilerParams(
-                collective_id=0, has_side_effects=True, vmem_limit_bytes=60 * 2**20
+                collective_id=0, has_side_effects=True, vmem_limit_bytes=vlim * 2**20
             ),
             name="star_attention",
         )
-        return call(lengths, positions, q, k, v, q_scored, weight)
+        context_out, scored_t = call(*[pltpu.with_memory_space_constraint(a, pltpu.HBM) for a in (lengths, positions, q, k, v, q_scored, weight.T)])
+        return context_out, scored_t.T
 
     in_specs = (P("blk", "tp"), P("blk", "tp"), P("blk", "tp"), P(), P("blk", "tp"), P("blk"), P("tp", "blk"))
     out_specs = (P("blk", "tp"), P("tp", "blk"))

time: 109 us -> 86.2 us (0.79)
  Pallas kernels: 102 us -> 83.4 us
  local copies, waits for them, and re-layouts: 6.27 us -> 1.93 us
    pallas_call x1, Pallas kernels: 102 us -> 83.4 us  [local(): call(*[pltpu.with_memory_space_constraint(a, pltpu.HBM) for a in (lengths...]
    unnamed x2, local copies, waits for them, and re-layouts: 4.82 us -> 1.93 us
    pallas_call x1 -> x0, local copies, waits for them, and re-layouts: 1.45 us -> none  [local(): return call(lengths, positions, q, k, v, q_scored, weight)]
where the time goes in v2:
time: 86.2 us; the launch traced here: 86 us
  Pallas kernels  83.4 us (97%)
  local copies, waits for them, and re-layouts  1.93 us (2%)
    pallas_call x1, Pallas kernels, local(): call(*[pltpu.with_memory_space_constraint(a, pltpu.HBM) for a in (lengths...  83.4 us
    unnamed x2, local copies, waits for them, and re-layouts  1.93 us

profile of v2, /device:TPU:1, one launch (start us, length us, event | category | flops | bytes accessed | tf_op | source)
XLA Modules:
  0.0 86.0 jit_solution(9160277487228623462)
XLA Ops:
  0.6 83.4 %star_attention.1 = (bf16[1024,1024]{1,0:T(8,128)(2,1)S(1)}, bf16[64,128]{1,0:T(8,128)(2,1)S(1)}) custom-call(s32[64]{0:T(128)} %lengths_hbm.1, s32[8]{0:T(128)} %positions_hbm.1, bf16[1024,1024]{1,0:T(8,128)(2,1)} %q_hbm.1, bf16[1024,256]{1,0:T(8,128)(2,1)} %k_hbm.1, bf16[1024,256]{1,0:T(8,128)(2,1)} %v_hbm.1, bf16[8,1024]{1,0:T(8,128)(2,1)} %qs_hbm.1, ...), custom_call_target="tpu_custom_call" | custom-call | tf_op jit(solution)/shard_map/star_attention/pallas_call | solution.py:847
  84.0 1.3 %copy.11 = bf16[1024,1024]{1,0:T(8,128)(2,1)} copy(bf16[1024,1024]{1,0:T(8,128)(2,1)S(1)} %get-tuple-element.8) | data formatting | bytes 4194304
  85.4 0.6 copy.12

commit v3 on v2

--- a/solution.py
+++ b/solution.py
@@ -204,6 +204,16 @@
             src_ref=src, dst_ref=dst, send_sem=send_sems.at[pair], recv_sem=recv_sems.at[pair], device_id=device, device_id_type=MESH
         )
 
+    def copy_to(src, dst, send, recv, device):
+        return pltpu.make_async_remote_copy(
+            src_ref=src,
+            dst_ref=dst,
+            send_sem=send_sems.at[send],
+            recv_sem=recv_sems.at[recv],
+            device_id=device,
+            device_id_type=MESH,
+        )
+
     sent = []
 
     def start(make):
@@ -302,12 +312,14 @@
             copy(self.b(xh, slice(None)), self.b(other, slice(None)), self.p_bx, {"blk": at_x(other)}).wait_recv()
 
     gather_q = Queries()
-    gather_kv = Plane(lambda a, b: ak.at[a, b], lambda a, b: av.at[a, b])
+    gather_k = Plane(lambda a, b: ak.at[a, b, :, 0:HEAD], lambda a, b: ak.at[a, b, :, HEAD : 2 * HEAD])
     gather_w = Plane(lambda a, b: wt.at[a, b, :, 0:512], lambda a, b: wt.at[a, b, :, 512:1024])
-    p_plane = [[sems.take() for _ in range(NY)] for _ in range(NX)]
-    sems.used += 8
-    p_kv = (sems.take(), sems.take())
-    p_line = [(sems.take(), sems.take()) for _ in range(1, NZ)]
+    p_hand_k = [[sems.take() for _ in range(NY)] for _ in range(NX)]
+    p_pass_v = [[sems.take() for _ in range(NY)] for _ in range(NX)]
+    p_hand_v = [sems.take() for _ in range(NZ)]
+    p_pass_k = [sems.take() for _ in range(NZ)]
+    p_line_v = [sems.take() for _ in range(NZ)]
+    p_k, p_v = sems.take(), sems.take()
     p_att = [sems.take() for _ in range(1, NZ)]
     p_out = [sems.take() for _ in range(NX * NY * HT)]
     p_from = sems.used
@@ -325,11 +337,11 @@
         qz[z, g] = jnp.concatenate(
             [q_piece[:, (g * 4 + h) * HEAD : (g * 4 + h + 1) * HEAD] for h in range(4)], axis=0
         ).astype(BF16)
-    row = lax.broadcasted_iota(jnp.int32, (TOK, HEAD), 0)
-    tile = jnp.zeros((TOK, HEAD), jnp.int32)
+    row = lax.broadcasted_iota(jnp.int32, (1, HEAD), 1)
+    line_of = jnp.zeros((1, HEAD), jnp.int32)
     for i in range(TOK):
-        tile = jnp.where(row == i, positions[i], tile)
-    pos[xh, z, y] = tile
+        line_of = jnp.where(row == i, positions[i], line_of)
+    pos[xh, z, y] = line_of
 
     pl.semaphore_wait(barrier, near)
     gather_q.start_z()
@@ -338,60 +350,85 @@
     loads[2].wait()
     loads[3].wait()
 
-    share = BT // (NX * NY)
-
-    def hand(dx, dy):
-        rows = pl.ds(pl.multiple_of((dx * NY + dy) * share, share), share)
-        device = {"blk": dx * (NZ * NY) + dy}
-        return [
-            pltpu.make_async_remote_copy(
-                src_ref=src.at[rows],
-                dst_ref=dst.at[dx, dy],
-                send_sem=send_sems.at[p_plane[dx][dy] + n * 8],
-                recv_sem=recv_sems.at[p_kv[n]],
-                device_id=device,
-                device_id_type=MESH,
-            )
-            for n, (src, dst) in enumerate(((k_ref, ak), (v_ref, av)))
-        ]
+    share_k = BT // (NX * NY)
+    share_v = BT // NZ
+
+    def hand_k(dx, dy):
+        rows = pl.ds((dx * NY + dy) * share_k, share_k)
+        return copy_to(k_ref.at[rows], ak.at[dx, dy], p_hand_k[dx][dy], p_k, {"blk": dx * (NZ * NY) + dy})
+
+    def hand_v(i):
+        return copy_to(v_ref.at[pl.ds(i * share_v, share_v)], av.at[i], p_hand_v[i], p_v, {"blk": i * NY})
+
+    def pass_k(i):
+        return copy_to(ak.at[xh, y], ak.at[xh, y], p_pass_k[i], p_k, {"blk": at_z(zs[i])})
+
+    def pass_v(dx, dy):
+        return copy_to(av.at[z], av.at[z], p_pass_v[dx][dy], p_v, {"blk": at_xy(dx, dy)})
+
+    def line_v(i):
+        return copy(av.at[z], av.at[z], p_line_v[i], {"blk": at_z(zs[i])})
+
+    plane = [(dx, dy) for dx in range(NX) for dy in range(NY) if dx or dy]
+    is_head = (xh == 0) & (y == 0)
 
     @pl.when(is_root)
     def _():
-        ak[0, 0] = k_ref[0:share, :]
-        av[0, 0] = v_ref[0:share, :]
-        for dx in range(NX):
-            for dy in range(NY):
-                if dx or dy:
-                    for c in hand(dx, dy):
-                        c.start()
-
-    def line(i):
-        return [
-            pltpu.make_async_remote_copy(
-                src_ref=ref.at[xh, y],
-                dst_ref=ref.at[xh, y],
-                send_sem=send_sems.at[p_line[i - 1][n]],
-                recv_sem=recv_sems.at[p_kv[n]],
-                device_id={"blk": at_z(zs[i])},
-                device_id_type=MESH,
-            )
-            for n, ref in enumerate((ak, av))
-        ]
-
-    def arrived():
-        for c in line(1):
-            c.wait_recv()
-
-    def pass_on():
+        ak[0, 0] = k_ref[0:share_k, :]
+        av[0] = v_ref[0:share_v, :]
+        for dx, dy in plane:
+            hand_k(dx, dy).start()
+        for i in range(1, NZ):
+            hand_v(i).start()
+
+    def pass_on_k():
         @pl.when((z == 0) & (blk > 0))
         def _():
-            arrived()
+            pass_k(1).wait_recv()
 
         @pl.when(z == 0)
         def _():
             for i in range(1, NZ):
-                for c in line(i):
-                    c.start()
+                pass_k(i).start()
+
+    def pass_on_v():
+        @pl.when(is_head & (z > 0))
+        def _():
+            pass_v(0, 1).wait_recv()
+
+        @pl.when(is_head)
+        def _():
+            for dx, dy in plane:
+                pass_v(dx, dy).start()
+
+    def gather_v():
+        @pl.when(jnp.logical_not(is_head))
+        def _():
+            pass_v(0, 1).wait_recv()
+
+        for i in range(1, NZ):
+            line_v(i).start()
+
+    def settle_kv():
+        @pl.when(is_root)
+        def _():
+            for dx, dy in plane:
+                hand_k(dx, dy).wait_send()
+            for i in range(1, NZ):
+                hand_v(i).wait_send()
+
+        @pl.when(z == 0)
+        def _():
+            for i in range(1, NZ):
+                pass_k(i).wait_send()
+
+        @pl.when(is_head)
+        def _():
+            for dx, dy in plane:
+                pass_v(dx, dy).wait_send()
+
+        for i in range(1, NZ):
+            line_v(i).wait_send()
 
     loads[6].wait()
     own_len = lengths[blk]
@@ -439,7 +476,7 @@
             if at_t == t:
                 pl.when(g == at_g)(hook)
 
-    own_hooks = {(0, 4): second_step, (1, 2): pass_on}
+    own_hooks = {(0, 4): second_step, (1, 2): pass_on_k, (1, 4): pass_on_v}
     lax.fori_loop(0, 2, own_group, 0)
     gather_q.wait_2()
     gather_q.start_3()
@@ -452,10 +489,18 @@
     rows0 = dev0 * PIECE
     rows1 = dev1 * PIECE
 
+    def limits_of(rows, count):
+        pick = lax.broadcasted_iota(jnp.int32, (count, TOK, HEAD), 1) == lax.broadcasted_iota(
+            jnp.int32, (count, TOK, HEAD), 2
+        )
+        spread = jnp.where(pick, jnp.broadcast_to(rows.astype(F32), (count, TOK, HEAD)), 0.0)
+        spread = jnp.broadcast_to(jnp.sum(spread, axis=2, keepdims=True), (count, TOK, HEAD))
+        return spread.astype(jnp.int32) - blk * BT
+
     def scored_scores(q, limits, g, slot, count):
         rows = count * PIECE
         q = jnp.concatenate([q, q], axis=1)
-        limits = jnp.concatenate([limits, limits], axis=2) - blk * BT
+        limits = jnp.concatenate([limits, limits], axis=2)
         m = jnp.full((rows, HEAD), NEG, F32)
         for c in range(BT // CHUNK):
             cols = slice(c * CHUNK, (c + 1) * CHUNK)
@@ -482,12 +527,12 @@
         out = jnp.full((TOK, HEAD), NEG, F32)
         for d, offset in zip(devices, offsets):
             for h in range(4):
-                out = jnp.where((lane == offset + h) & (limits[d] >= blk * BT), lse[d, h], out)
+                out = jnp.where((lane == offset + h) & (limits[d] >= 0), lse[d, h], out)
         return out
 
     def scored_0(i):
         yi = yb[i]
-        lim0 = pos[:, :, yi].reshape(dev0, TOK, HEAD)
+        lim0 = limits_of(pos[:, :, yi].reshape(dev0, 1, HEAD), dev0)
         peak0 = scored_scores(qa[:, :, yi].reshape(rows0, HEAD), lim0, 0, 0, dev0)
         out0, lse0 = scored_values(peak0, 0, 0, dev0)
         o0[yi] = out0.reshape(NX, NZ, PIECE, HEAD)
@@ -500,7 +545,7 @@
     def scored_1(i):
         xi = xh if i < halves else other
         z0 = (i % halves) * zpart
-        lim1 = pos1[xi, z0 : z0 + zpart].reshape(dev1, TOK, HEAD)
+        lim1 = limits_of(pos1[xi, z0 : z0 + zpart].reshape(dev1, 1, HEAD), dev1)
         peak1 = scored_scores(qb[xi, z0 : z0 + zpart].reshape(rows1, HEAD), lim1, 1, 1, dev1)
         out1, lse1 = scored_values(peak1, 1, 1, dev1)
         o1[xi, z0 : z0 + zpart] = out1.reshape(zpart, NY, PIECE, HEAD)
@@ -516,20 +561,20 @@
     scored_0(0)
     for i in range(halves):
         scored_1(i)
+    pl.when(z > 0)(lambda: pass_k(1).wait_recv())
+    gather_k.start_1()
+    gather_v()
     order = [1, 3, 2] if NY == 4 else list(range(1, NY))
     for n, i in enumerate(order):
         gather_q.wait_3y(i)
         scored_0(i)
-        if n == 0:
-            pl.when(z > 0)(arrived)
-            gather_kv.start_1()
     gather_q.wait_3x()
     for i in range(halves, NY):
         scored_1(i)
         send_1(i - halves)
     start(lambda: copy(st1.at[other], t1x, p_x1[halves], {"blk": at_x(other)}))
-    gather_kv.wait_1()
-    gather_kv.start_2()
+    gather_k.wait_1()
+    gather_k.start_2()
 
     def sums_1():
         for i in range(1, NY):
@@ -567,7 +612,7 @@
             return jnp.where(xh == 0, t, pltpu.roll(t, 64, 1))
 
         ws, lse = merge([own_x(l0x[...]), own_x(t0x[...])])
-        lz[0] = lse
+        lse0 = lse
         for b in range(NZ):
             total = o0x[xh, b].astype(F32) * lane_weights(ws[0], b * 8)
             total += r0x[b].astype(F32) * lane_weights(ws[1], b * 8)
@@ -576,7 +621,7 @@
             copy(o1y.at[y], r1y.at[i - 1], p_y1[i - 1][0], {"blk": at_y(ys[i])}).wait_recv()
             copy(l1y.at[y], t1y.at[i - 1], p_y1[i - 1][1], {"blk": at_y(ys[i])}).wait_recv()
         ws, lse = merge([l1y[y]] + [t1y[i] for i in range(NY - 1)])
-        lz[1] = lse
+        lz[...] = jnp.where(lax.rem(lane, 8) < 4, lse0, pltpu.roll(lse, 4, 1))
         for b in range(NZ):
             total = o1y[y, b].astype(F32) * lane_weights(ws[0], b * 8)
             for i in range(NY - 1):
@@ -590,15 +635,15 @@
         for i in range(1, NZ):
             copy(oz.at[z], rz.at[i - 1], p_z01[i - 1][0], {"blk": at_z(zs[i])}).wait_recv()
             copy(lz, tz.at[i - 1], p_z01[i - 1][1], {"blk": at_z(zs[i])}).wait_recv()
+        ws, _ = merge([lz[...]] + [tz[i] for i in range(NZ - 1)])
         for g in range(2):
-            ws, _ = merge([lz[g]] + [tz[i, g] for i in range(NZ - 1)])
             total = jnp.zeros((PIECE, HEAD), F32)
             for i in range(NZ):
                 part = oz[z, g] if i == 0 else rz[i - 1, g]
                 factor = jnp.concatenate(
                     [
                         jnp.broadcast_to(
-                            jnp.sum(jnp.where(lane == z * 8 + h, ws[i], 0.0), axis=1, keepdims=True), (TOK, HEAD)
+                            jnp.sum(jnp.where(lane == z * 8 + g * 4 + h, ws[i], 0.0), axis=1, keepdims=True), (TOK, HEAD)
                         )
                         for h in range(4)
                     ],
@@ -702,17 +747,25 @@
                     else:
                         pl.when(xh * HT + n != tp)(settle)
 
+    def weights_2():
+        sums_2()
+        gather_w.wait_1()
+        gather_w.start_2()
+
+    def attended():
+        sums_3()
+        stores[0].start()
+
     sums_1()
-    sums_2()
-    gather_kv.wait_2()
-    gather_w.wait_1()
-    gather_w.start_2()
+    gather_k.wait_2()
+    for i in range(1, NZ):
+        copy(av.at[z], av.at[zb[i]], p_line_v[i], {"blk": at_z(zs[i])}).wait_recv()
     expand_keys(ak[...].reshape(BT, 2 * HEAD), av[...].reshape(BT, 2 * HEAD), anchor_len, k_ref, akx, avx)
     stores = [
         pltpu.make_async_copy(out_buf.at[g], ctx_hbm.at[:, g * 512 : (g + 1) * 512], local_sems.at[3 + g])
         for g in range(2)
     ]
-    anchor_hooks = {(0, 2): sums_3, (1, 0): stores[0].start, (1, 2): project}
+    anchor_hooks = {(0, 2): weights_2, (1, 0): attended, (1, 3): project}
 
     def anchor_group(g, carry):
         prev = None
@@ -753,20 +806,7 @@
     for make in sent:
         make().wait_send()
 
-    @pl.when(is_root)
-    def _():
-        for dx in range(NX):
-            for dy in range(NY):
-                if dx or dy:
-                    for c in hand(dx, dy):
-                        c.wait_send()
-
-    @pl.when(z == 0)
-    def _():
-        for i in range(1, NZ):
-            for c in line(i):
-                c.wait_send()
-
+    settle_kv()
     for c in stores:
         c.wait()
 
@@ -807,10 +847,10 @@
                 pltpu.VMEM((NZ, 2, PIECE, HEAD), BF16),
                 pltpu.VMEM(pieces, BF16),
                 pltpu.VMEM(pieces, BF16),
-                pltpu.VMEM((NX, NZ, NY, TOK, HEAD), jnp.int32),
-                pltpu.VMEM((NX, NZ, NY, TOK, HEAD), jnp.int32),
+                pltpu.VMEM((NX, NZ, NY, 1, HEAD), jnp.int32),
+                pltpu.VMEM((NX, NZ, NY, 1, HEAD), jnp.int32),
                 pltpu.VMEM(anchor, BF16),
-                pltpu.VMEM(anchor, BF16),
+                pltpu.VMEM((NZ, BT // NZ, 2 * HEAD), BF16),
                 pltpu.VMEM((NY, NX, NZ, PIECE, HEAD), BF16),
                 pltpu.VMEM((NX, NZ, NY, PIECE, HEAD), BF16),
                 pltpu.VMEM((NY, TOK, HEAD), F32),
@@ -828,15 +868,15 @@
                 pltpu.VMEM((NY - 1, NZ, PIECE, HEAD), BF16),
                 pltpu.VMEM((NY - 1, TOK, HEAD), F32),
                 pltpu.VMEM((NZ, 2, PIECE, HEAD), BF16),
-                pltpu.VMEM((2, TOK, HEAD), F32),
+                pltpu.VMEM((TOK, HEAD), F32),
                 pltpu.VMEM((NZ - 1, 2, PIECE, HEAD), BF16),
-                pltpu.VMEM((NZ - 1, 2, TOK, HEAD), F32),
+                pltpu.VMEM((NZ - 1, TOK, HEAD), F32),
                 pltpu.VMEM((NZ, 2, PIECE, HEAD), BF16),
                 pltpu.VMEM((NX, NY, 64, 1024), BF16),
                 pltpu.VMEM((NX * NY, NT // NX, NZ * NX // NT * TOK // 2, HEAD), BF16),
                 pltpu.VMEM((NY, NT, NZ * NX // NT * TOK // 2, HEAD), BF16),
-                pltpu.SemaphoreType.DMA((200,)),
-                pltpu.SemaphoreType.DMA((200,)),
+                pltpu.SemaphoreType.DMA((240,)),
+                pltpu.SemaphoreType.DMA((240,)),
                 pltpu.SemaphoreType.DMA((9,)),
             ],
             compiler_params=pltpu.CompilerParams(
@@ -844,7 +884,8 @@
             ),
             name="star_attention",
         )
-        context_out, scored_t = call(*[pltpu.with_memory_space_constraint(a, pltpu.HBM) for a in (lengths, positions, q, k, v, q_scored, weight.T)])
+        arrays = (lengths, positions, q, k, v, q_scored, weight.T)
+        context_out, scored_t = call(*[pltpu.with_memory_space_constraint(a, pltpu.HBM) for a in arrays])
         return context_out, scored_t.T
 
     in_specs = (P("blk", "tp"), P("blk", "tp"), P("blk", "tp"), P(), P("blk", "tp"), P("blk"), P("tp", "blk"))

time: 86.2 us -> 76.2 us (0.88)
  Pallas kernels: 83.4 us -> 73.5 us
    pallas_call x1, Pallas kernels: 83.4 us -> 73.5 us  [local(): call(*[pltpu.with_memory_space_constraint(a, pltpu.HBM) for a in arrays])]
where the time goes in v3:
time: 76.2 us; the launch traced here: 76.1 us
  Pallas kernels  73.5 us (96%)
  local copies, waits for them, and re-layouts  1.93 us (3%)
    pallas_call x1, Pallas kernels, local(): call(*[pltpu.with_memory_space_constraint(a, pltpu.HBM) for a in arrays])  73.5 us
    unnamed x2, local copies, waits for them, and re-layouts  1.93 us

profile of v3, /device:TPU:1, one launch (start us, length us, event | category | flops | bytes accessed | tf_op | source)
XLA Modules:
  0.0 76.1 jit_solution(311842293940437292)
XLA Ops:
  0.6 73.5 %star_attention.1 = (bf16[1024,1024]{1,0:T(8,128)(2,1)S(1)}, bf16[64,128]{1,0:T(8,128)(2,1)S(1)}) custom-call(s32[64]{0:T(128)} %lengths_hbm.1, s32[8]{0:T(128)} %positions_hbm.1, bf16[1024,1024]{1,0:T(8,128)(2,1)} %q_hbm.1, bf16[1024,256]{1,0:T(8,128)(2,1)} %k_hbm.1, bf16[1024,256]{1,0:T(8,128)(2,1)} %v_hbm.1, bf16[8,1024]{1,0:T(8,128)(2,1)} %qs_hbm.1, ...), custom_call_target="tpu_custom_call" | custom-call | tf_op jit(solution)/shard_map/star_attention/pallas_call | solution.py:888
  74.1 1.3 %copy.11 = bf16[1024,1024]{1,0:T(8,128)(2,1)} copy(bf16[1024,1024]{1,0:T(8,128)(2,1)S(1)} %get-tuple-element.8) | data formatting | bytes 4194304
  75.5 0.6 copy.12

commit v4 on v3

--- a/solution.py
+++ b/solution.py
@@ -111,18 +111,10 @@
     o1,
     st0,
     st1,
-    r0y,
-    t0y,
-    r1x,
-    t1x,
-    o0x,
-    l0x,
-    r0x,
-    t0x,
-    o1y,
-    l1y,
-    r1y,
-    t1y,
+    r0,
+    t0,
+    r1,
+    t1,
     oz,
     lz,
     rz,
@@ -324,10 +316,7 @@
     p_out = [sems.take() for _ in range(NX * NY * HT)]
     p_from = sems.used
     sems.used += NY * NT
-    p_y0 = [(sems.take(), sems.take()) for _ in range(1, NY)]
-    p_x1 = [sems.take() for _ in range(NY // NX + 1)]
-    p_x0 = [(sems.take(), sems.take())]
-    p_y1 = [(sems.take(), sems.take()) for _ in range(1, NY)]
+    p_sum = [[sems.take() for _ in range(4)] for _ in range(NX * NY)]
     p_z01 = [(sems.take(), sems.take()) for _ in range(1, NZ)]
 
     loads[0].wait()
@@ -537,11 +526,6 @@
         out0, lse0 = scored_values(peak0, 0, 0, dev0)
         o0[yi] = out0.reshape(NX, NZ, PIECE, HEAD)
         st0[yi] = stat_tile(lse0, lim0, range(dev0), [(d // NZ) * 64 + (d % NZ) * 8 for d in range(dev0)])
-        if i > 0:
-            pairs = p_y0[NY - i - 1]
-            start(lambda pair=pairs[0]: copy(o0.at[yi], r0y.at[NY - i - 1], pair, {"blk": at_y(yi)}))
-            start(lambda pair=pairs[1]: copy(st0.at[yi], t0y.at[NY - i - 1], pair, {"blk": at_y(yi)}))
-
     def scored_1(i):
         xi = xh if i < halves else other
         z0 = (i % halves) * zpart
@@ -554,9 +538,14 @@
             new = stat_tile(lse1, lim1, devices, [(z0 + zz) * 8 for zz in range(zpart)])
             st1[xi, yy] = new if i % halves == 0 else jnp.maximum(st1[xi, yy], new)
 
-    def send_1(n):
-        at = slice(n * zpart, (n + 1) * zpart)
-        start(lambda: copy(o1.at[other, at], r1x.at[at], p_x1[n], {"blk": at_x(other)}))
+    def send_sum(g, dx, dy):
+        k = dx * NY + dy
+        if g == 0:
+            parts = lambda: ((o0.at[ys[dy], xs[dx]], r0.at[k]), (st0.at[ys[dy]], t0.at[k]))
+        else:
+            parts = lambda: ((o1.at[xs[dx], :, ys[dy]], r1.at[k]), (st1.at[xs[dx], ys[dy]], t1.at[k]))
+        for n in range(2):
+            start(lambda n=n: copy(*parts()[n], p_sum[k][2 * g + n], {"blk": at_xy(dx, dy)}))
 
     scored_0(0)
     for i in range(halves):
@@ -568,65 +557,44 @@
     for n, i in enumerate(order):
         gather_q.wait_3y(i)
         scored_0(i)
+        for dx in range(NX):
+            send_sum(0, dx, NY - i)
     gather_q.wait_3x()
+    send_sum(0, 1, 0)
+    for dy in range(1, NY):
+        send_sum(1, 0, dy)
     for i in range(halves, NY):
         scored_1(i)
-        send_1(i - halves)
-    start(lambda: copy(st1.at[other], t1x, p_x1[halves], {"blk": at_x(other)}))
+    for dy in range(NY):
+        send_sum(1, 1, dy)
     gather_k.wait_1()
     gather_k.start_2()
 
-    def sums_1():
-        for i in range(1, NY):
-            copy(o0.at[y], r0y.at[i - 1], p_y0[i - 1][0], {"blk": at_y(ys[i])}).wait_recv()
-            copy(st0.at[y], t0y.at[i - 1], p_y0[i - 1][1], {"blk": at_y(ys[i])}).wait_recv()
-        ws, l0x[...] = merge([st0[y]] + [t0y[i] for i in range(NY - 1)])
-        for a in range(NX):
-            for b in range(NZ):
-                at = a * 64 + b * 8
-                total = o0[y, a, b].astype(F32) * lane_weights(ws[0], at)
-                for i in range(NY - 1):
-                    total += r0y[i, a, b].astype(F32) * lane_weights(ws[i + 1], at)
-                o0x[a, b] = total.astype(BF16)
-        start(lambda: copy(o0x.at[other], r0x, p_x0[0][0], {"blk": at_x(other)}))
-        start(lambda: copy(l0x, t0x, p_x0[0][1], {"blk": at_x(other)}))
-        for n in range(halves):
-            at = slice(n * zpart, (n + 1) * zpart)
-            copy(o1.at[xh, at], r1x.at[at], p_x1[n], {"blk": at_x(other)}).wait_recv()
-        copy(st1.at[xh], t1x, p_x1[halves], {"blk": at_x(other)}).wait_recv()
-        for c in range(NY):
-            ws, l1y[c] = merge([st1[xh, c], t1x[c]])
-            for b in range(NZ):
-                total = o1[xh, b, c].astype(F32) * lane_weights(ws[0], b * 8)
-                total += r1x[b, c].astype(F32) * lane_weights(ws[1], b * 8)
-                o1y[c, b] = total.astype(BF16)
-        for i in range(1, NY):
-            start(lambda i=i: copy(o1y.at[ys[i]], r1y.at[i - 1], p_y1[i - 1][0], {"blk": at_y(ys[i])}))
-            start(lambda i=i: copy(l1y.at[ys[i]], t1y.at[i - 1], p_y1[i - 1][1], {"blk": at_y(ys[i])}))
-
-    def sums_2():
-        copy(o0x.at[xh], r0x, p_x0[0][0], {"blk": at_x(other)}).wait_recv()
-        copy(l0x, t0x, p_x0[0][1], {"blk": at_x(other)}).wait_recv()
+    def sums_12():
+        for dx, dy in plane:
+            k = dx * NY + dy
+            pairs = (
+                (o0.at[y, xh], r0.at[k]),
+                (st0.at[y], t0.at[k]),
+                (o1.at[xh, :, y], r1.at[k]),
+                (st1.at[xh, y], t1.at[k]),
+            )
+            for n, (src, dst) in enumerate(pairs):
+                copy(src, dst, p_sum[k][n], {"blk": at_x(other)}).wait_recv()
+        slots = [dx * NY + dy for dx, dy in plane]
 
         def own_x(t):
             return jnp.where(xh == 0, t, pltpu.roll(t, 64, 1))
 
-        ws, lse = merge([own_x(l0x[...]), own_x(t0x[...])])
-        lse0 = lse
+        ws0, lse0 = merge([own_x(t) for t in [st0[y]] + [t0[k] for k in slots]])
+        ws1, lse1 = merge([st1[xh, y]] + [t1[k] for k in slots])
+        lz[...] = jnp.where(lax.rem(lane, 8) < 4, lse0, pltpu.roll(lse1, 4, 1))
         for b in range(NZ):
-            total = o0x[xh, b].astype(F32) * lane_weights(ws[0], b * 8)
-            total += r0x[b].astype(F32) * lane_weights(ws[1], b * 8)
-            oz[b, 0] = total.astype(BF16)
-        for i in range(1, NY):
-            copy(o1y.at[y], r1y.at[i - 1], p_y1[i - 1][0], {"blk": at_y(ys[i])}).wait_recv()
-            copy(l1y.at[y], t1y.at[i - 1], p_y1[i - 1][1], {"blk": at_y(ys[i])}).wait_recv()
-        ws, lse = merge([l1y[y]] + [t1y[i] for i in range(NY - 1)])
-        lz[...] = jnp.where(lax.rem(lane, 8) < 4, lse0, pltpu.roll(lse, 4, 1))
-        for b in range(NZ):
-            total = o1y[y, b].astype(F32) * lane_weights(ws[0], b * 8)
-            for i in range(NY - 1):
-                total += r1y[i, b].astype(F32) * lane_weights(ws[i + 1], b * 8)
-            oz[b, 1] = total.astype(BF16)
+            for g, ws, mine, theirs in ((0, ws0, o0[y, xh, b], r0), (1, ws1, o1[xh, b, y], r1)):
+                total = mine.astype(F32) * lane_weights(ws[0], b * 8)
+                for n, k in enumerate(slots):
+                    total += theirs[k, b].astype(F32) * lane_weights(ws[n + 1], b * 8)
+                oz[b, g] = total.astype(BF16)
         for i in range(1, NZ):
             start(lambda i=i: copy(oz.at[zs[i]], rz.at[i - 1], p_z01[i - 1][0], {"blk": at_z(zs[i])}))
             start(lambda i=i: copy(lz, tz.at[i - 1], p_z01[i - 1][1], {"blk": at_z(zs[i])}))
@@ -748,15 +716,11 @@
                         pl.when(xh * HT + n != tp)(settle)
 
     def weights_2():
-        sums_2()
+        sums_12()
         gather_w.wait_1()
         gather_w.start_2()
 
-    def attended():
-        sums_3()
-        stores[0].start()
-
-    sums_1()
+    weights_2()
     gather_k.wait_2()
     for i in range(1, NZ):
         copy(av.at[z], av.at[zb[i]], p_line_v[i], {"blk": at_z(zs[i])}).wait_recv()
@@ -765,7 +729,7 @@
         pltpu.make_async_copy(out_buf.at[g], ctx_hbm.at[:, g * 512 : (g + 1) * 512], local_sems.at[3 + g])
         for g in range(2)
     ]
-    anchor_hooks = {(0, 2): weights_2, (1, 0): attended, (1, 3): project}
+    anchor_hooks = {(0, 2): sums_3, (1, 0): stores[0].start, (1, 1): project}
 
     def anchor_group(g, carry):
         prev = None
@@ -855,18 +819,10 @@
                 pltpu.VMEM((NX, NZ, NY, PIECE, HEAD), BF16),
                 pltpu.VMEM((NY, TOK, HEAD), F32),
                 pltpu.VMEM((NX, NY, TOK, HEAD), F32),
-                pltpu.VMEM((NY - 1, NX, NZ, PIECE, HEAD), BF16),
-                pltpu.VMEM((NY - 1, TOK, HEAD), F32),
-                pltpu.VMEM((NZ, NY, PIECE, HEAD), BF16),
-                pltpu.VMEM((NY, TOK, HEAD), F32),
-                pltpu.VMEM((NX, NZ, PIECE, HEAD), BF16),
-                pltpu.VMEM((TOK, HEAD), F32),
-                pltpu.VMEM((NZ, PIECE, HEAD), BF16),
-                pltpu.VMEM((TOK, HEAD), F32),
-                pltpu.VMEM((NY, NZ, PIECE, HEAD), BF16),
-                pltpu.VMEM((NY, TOK, HEAD), F32),
-                pltpu.VMEM((NY - 1, NZ, PIECE, HEAD), BF16),
-                pltpu.VMEM((NY - 1, TOK, HEAD), F32),
+                pltpu.VMEM((NX * NY, NZ, PIECE, HEAD), BF16),
+                pltpu.VMEM((NX * NY, TOK, HEAD), F32),
+                pltpu.VMEM((NX * NY, NZ, PIECE, HEAD), BF16),
+                pltpu.VMEM((NX * NY, TOK, HEAD), F32),
                 pltpu.VMEM((NZ, 2, PIECE, HEAD), BF16),
                 pltpu.VMEM((TOK, HEAD), F32),
                 pltpu.VMEM((NZ - 1, 2, PIECE, HEAD), BF16),

time: 76.2 us -> 74.3 us (0.975)
  Pallas kernels: 73.5 us -> 70.9 us
    pallas_call x1, Pallas kernels: 73.5 us -> 70.9 us  [local(): call(*[pltpu.with_memory_space_constraint(a, pltpu.HBM) for a in arrays])]
where the time goes in v4:
time: 74.3 us; the launch traced here: 73.5 us
  Pallas kernels  70.9 us (95%)
  local copies, waits for them, and re-layouts  1.93 us (3%)
    pallas_call x1, Pallas kernels, local(): call(*[pltpu.with_memory_space_constraint(a, pltpu.HBM) for a in arrays])  70.9 us
    unnamed x2, local copies, waits for them, and re-layouts  1.93 us

profile of v4, /device:TPU:1, one launch (start us, length us, event | category | flops | bytes accessed | tf_op | source)
XLA Modules:
  0.0 73.5 jit_solution(5741219538790073958)
XLA Ops:
  0.6 70.9 %star_attention.1 = (bf16[1024,1024]{1,0:T(8,128)(2,1)S(1)}, bf16[64,128]{1,0:T(8,128)(2,1)S(1)}) custom-call(s32[64]{0:T(128)} %lengths_hbm.1, s32[8]{0:T(128)} %positions_hbm.1, bf16[1024,1024]{1,0:T(8,128)(2,1)} %q_hbm.1, bf16[1024,256]{1,0:T(8,128)(2,1)} %k_hbm.1, bf16[1024,256]{1,0:T(8,128)(2,1)} %v_hbm.1, bf16[8,1024]{1,0:T(8,128)(2,1)} %qs_hbm.1, ...), custom_call_target="tpu_custom_call" | custom-call | tf_op jit(solution)/shard_map/star_attention/pallas_call | solution.py:844
  71.5 1.3 %copy.11 = bf16[1024,1024]{1,0:T(8,128)(2,1)} copy(bf16[1024,1024]{1,0:T(8,128)(2,1)S(1)} %get-tuple-element.8) | data formatting | bytes 4194304
  72.8 0.6 copy.12
